TPU v7x, 512 devices: a whole 4x8x8 slice. The times are simulated.
512 devices in a mesh: band: 256 (over y, x_hi, z, core), grid: 2 (over x_lo).
Axes of the slice: x: 4 (x_hi: 2, x_lo: 2; x = x_hi * 2 + x_lo), y: 8, z: 8, core: 2. Of those that a mesh axis runs over, the one named last changes fastest.
Arguments:
- orbitals: float32 [256, 64, 4096], P('band', 'grid'), may hold values from -1.8 to 1.8
Outputs:
- exchange_partial: float32 [256, 64, 4096], P('band', 'grid')
All inputs are finite; a program needn't handle non-finite values.
Results may differ from a plain program's by a relative error of at most 0.0044.
Values may be sent and summed in bfloat16 or wider, within the bound.
No kernel may reach another device: no remote copies, remote signals or barrier semaphores. Data moves between devices by JAX's collectives and lax.ppermute only.
A program may use at most 64 MiB of HBM per device.

v0:
```python
import math

import jax
import jax.numpy as jnp
import numpy as np
from jax import lax
from jax.experimental import pallas as pl
from jax.experimental.pallas import tpu as pltpu
from jax.sharding import PartitionSpec as P

NG = 64
REACH = 2
NEAR = 0
ROWS = NG // 2
PLANE = NG * NG
LANES = 2 * NG
BLOCKS = PLANE // LANES
CODE = 64.0
CHUNK = 8
WIDTH = 1024
coulomb = 46.9 * 46.9 / math.pi


def cas_table():
    count = np.arange(NG)
    angle = 2.0 * math.pi / NG * (count[:, None] * count[None, :] % NG)
    return np.cos(angle) + np.sin(angle)


def split(table):
    high = table.astype(jnp.bfloat16)
    low = (table - high.astype(np.float64)).astype(jnp.bfloat16)
    return high, low


def plane_matrix():
    cas = cas_table()
    high, low = split(np.block([[cas, cas], [cas, -cas]]))
    return np.concatenate([high, low], axis=1)


def x_matrices():
    cas = cas_table()
    high, low = split(cas)
    return high, np.concatenate([high, high, low], axis=1)


def kernel_table():
    count = np.arange(NG)
    folded = np.where(count < NG // 2, count, count - NG)
    square = (folded * folded).astype(np.float64)
    block, upper, last = np.meshgrid(
        np.arange(BLOCKS), np.arange(2), np.arange(NG), indexing="ij"
    )
    column = (square[block + BLOCKS * upper] + square[last]).reshape(1, PLANE)
    msq = square[:, None] + column
    table = np.where(msq > 0.0, coulomb / np.maximum(msq, 1.0), 0.0) / NG**3
    return table.astype(np.float32)


def hartley(items):
    n = len(items)
    if n == 1:
        return items
    even, odd = hartley(items[0::2]), hartley(items[1::2])
    half = n // 2
    turned = list(odd)
    for k in range(1, (half + 1) // 2):
        c, s = math.cos(2.0 * math.pi * k / n), math.sin(2.0 * math.pi * k / n)
        a, b = odd[k], odd[half - k]
        if 8 * k == n:
            turned[k], turned[half - k] = (a + b) * c, (a - b) * c
        else:
            turned[k], turned[half - k] = a * c + b * s, a * s - b * c
    return [e + t for e, t in zip(even, turned)] + [e - t for e, t in zip(even, turned)]


def twist(items):
    n = len(items)
    low_lanes = lax.broadcasted_iota(jnp.int32, items[0].shape, 1) < NG
    out = [None] * n
    out[0] = items[0]
    for k in range(1, n // 2):
        c, s = math.cos(math.pi * k / n), math.sin(math.pi * k / n)
        a, b = items[k], items[n - k]
        out[k] = jnp.where(low_lanes, a, a * c + b * s)
        out[n - k] = jnp.where(low_lanes, b, a * s - b * c)
    out[n // 2] = items[n // 2]
    return out


def decoded(code):
    return jnp.log2(code.astype(jnp.float32)) * (1.0 / CODE)


def lane_block(b):
    return slice(b * LANES, (b + 1) * LANES)


def pairwise(items):
    while len(items) > 1:
        items = [a + b for a, b in zip(items[0::2], items[1::2])]
    return items[0]


def pairwise(items):
    while len(items) > 1:
        items = [a + b for a, b in zip(items[0::2], items[1::2])]
    return items[0]


def encode_kernel(psi_ref, code_ref, marked_ref):
    psi = psi_ref[0]
    code = jnp.exp2(psi * CODE).astype(jnp.bfloat16)
    code_ref[...] = code
    marked_ref[:, :PLANE] = code
    part = pairwise([psi[:, lane_block(b)] ** 2 for b in range(BLOCKS)])
    coarse = jnp.round(part * 512.0) * (1.0 / 512.0)
    total = jnp.sum(coarse, axis=1, keepdims=True) + jnp.sum(part - coarse, axis=1, keepdims=True)
    marked_ref[:, PLANE:] = jnp.broadcast_to(total, (ROWS, LANES)).astype(jnp.bfloat16)


def forward(mine, other, plane_ref, spec_ref, scratch):
    for tile in range(NG // 8):
        slab, row = divmod(8 * tile, ROWS)
        rows = slice(row, row + 8)
        fields = [
            mine[slab][rows, lane_block(b)] * other[slab][rows, lane_block(b)]
            for b in range(BLOCKS)
        ]
        for b, item in enumerate(twist(hartley(fields))):
            scratch[b * NG + 8 * tile : b * NG + 8 * tile + 8, :] = item
    for first in range(0, BLOCKS, CHUNK):
        value = scratch[first * NG : (first + CHUNK) * NG, :]
        high = value.astype(jnp.bfloat16)
        low = (value - high.astype(jnp.float32)).astype(jnp.bfloat16)
        operand = jnp.concatenate([high, low], axis=1)
        both = jnp.dot(operand, plane_ref[...], preferred_element_type=jnp.float32)
        spec = (both[:, :LANES] + both[:, LANES:]).astype(jnp.bfloat16)
        for b in range(CHUNK):
            spec_ref[:, lane_block(first + b)] = spec[b * NG : (b + 1) * NG]


def screen(spec_ref, low_ref, wide_ref, table_ref, rows):
    for first in range(0, PLANE, WIDTH):
        lanes = slice(first, first + WIDTH)
        value = jnp.dot(low_ref[...], spec_ref[:, lanes], preferred_element_type=jnp.float32)
        value = value * table_ref[:, lanes]
        high = value.astype(jnp.bfloat16)
        low = (value - high.astype(jnp.float32)).astype(jnp.bfloat16)
        operand = jnp.concatenate([high, low, high], axis=0)
        result = jnp.dot(wide_ref[:rows], operand, preferred_element_type=jnp.float32)
        spec_ref[:rows, lanes] = result.astype(jnp.bfloat16)


def inverse(spec_ref, plane_ref, scratch, rows, use):
    for first in range(0, BLOCKS, CHUNK):
        operand = jnp.concatenate(
            [spec_ref[:rows, lane_block(first + b)] for b in range(CHUNK)], axis=0
        )
        both = jnp.dot(operand, plane_ref[:LANES], preferred_element_type=jnp.float32)
        scratch[first * rows : (first + CHUNK) * rows, :] = both[:, :LANES] + both[:, LANES:]
    for tile in range(rows // 8):
        fields = [scratch[b * rows + 8 * tile : b * rows + 8 * tile + 8, :] for b in range(BLOCKS)]
        slab, row = divmod(8 * tile, ROWS)
        for b, item in enumerate(hartley(twist(fields))):
            use(slab, slice(row, row + 8), lane_block(b), item)


def copy_kernel(code_ref, out_ref):
    out_ref[...] = code_ref[...]


def self_kernel(psi_ref, mine_ref, beside_ref, plane_ref, low_ref, wide_ref, table_ref,
                beside_out, total_out, spec, scratch):
    beside_out[...] = decoded(beside_ref[:, :PLANE])
    band = (psi_ref.at[0], beside_out)
    forward(band, band, plane_ref, spec, scratch)
    first = lax.broadcasted_iota(jnp.int32, (ROWS, LANES), 1) == 0
    for rows, ref in ((slice(0, ROWS), mine_ref), (slice(ROWS, NG), beside_ref)):
        spec[rows, :LANES] = jnp.where(first, ref[:, PLANE:], spec[rows, :LANES])
    screen(spec, low_ref, wide_ref, table_ref, ROWS)

    def use(slab, rows, lanes, item):
        total_out[rows, lanes] = psi_ref[0, rows, lanes] * item

    inverse(spec, plane_ref, scratch, ROWS, use)


def pair_kernel(psi_ref, beside_ref, same_ref, cross_ref, plane_ref, low_ref, wide_ref,
                table_ref, part_ref, total_out, beside_out, same_out, cross_out,
                other, spec, scratch, sums):
    other[0] = decoded(same_ref[...])
    other[1] = decoded(cross_ref[...])
    band = (psi_ref.at[0], beside_ref)
    forward(band, (other.at[0], other.at[1]), plane_ref, spec, scratch)
    screen(spec, low_ref, wide_ref, table_ref, NG)

    def use(slab, rows, lanes, item):
        part = other[slab, rows, lanes] * item
        if slab == 0:
            total_out[rows, lanes] = part_ref[rows, lanes] + part
        else:
            sums[2, rows, lanes] = part
        sums[slab, rows, lanes] = band[slab][rows, lanes] * item

    inverse(spec, plane_ref, scratch, NG, use)
    same_out[...] = sums[0].astype(jnp.bfloat16)
    cross_out[...] = sums[1].astype(jnp.bfloat16)
    beside_out[...] = sums[2].astype(jnp.bfloat16)


vmem = pl.BlockSpec(memory_space=pltpu.VMEM)
limit = pltpu.CompilerParams(vmem_limit_bytes=40 * 1024 * 1024)


def shape(dims, dtype):
    return jax.ShapeDtypeStruct(dims, dtype)


def call(kernel, outs, *args, scratch=()):
    return pl.pallas_call(
        kernel, out_shape=outs, in_specs=[vmem] * len(args),
        out_specs=jax.tree.map(lambda _: vmem, outs),
        scratch_shapes=scratch, compiler_params=limit,
    )(*args)


def on_device(orbitals):
    bands = lax.axis_size("band")
    axes = ("band", "grid")

    def route(flip):
        pairs = []
        for band in range(bands):
            for g in range(2):
                other = (band - (1 if g == NEAR else REACH)) % bands
                pairs.append((2 * other + (1 - g if flip else g), 2 * band + g))
        return pairs

    def home(flip):
        return [(b, a) for a, b in route(flip)]

    swap = [(0, 1), (1, 0)]
    plane = jnp.asarray(plane_matrix())
    stacked = jnp.concatenate([plane, plane], axis=0)
    x_low, x_wide = (jnp.asarray(m) for m in x_matrices())
    table = jnp.asarray(kernel_table())
    tables = (stacked, x_low, x_wide, table)

    sent = shape((ROWS, PLANE), jnp.bfloat16)
    field = shape((ROWS, PLANE), jnp.float32)
    spec = pltpu.VMEM((NG, PLANE), jnp.bfloat16)
    work = pltpu.VMEM((BLOCKS * NG, LANES), jnp.float32)
    marks = shape((ROWS, PLANE + LANES), jnp.bfloat16)

    code, marked = call(encode_kernel, (sent, marks), orbitals)
    same = lax.ppermute(code, axes, route(False))
    cross = lax.ppermute(code, axes, route(True))
    marked = call(copy_kernel, marks, marked)
    beside = lax.ppermute(marked, "grid", swap)
    beside, total = call(
        self_kernel, (field, field), orbitals, marked, beside, *tables, scratch=[spec, work]
    )
    total, beside, same, cross = call(
        pair_kernel, (field, sent, sent, sent),
        orbitals, beside, same, cross, *tables, total,
        scratch=[
            pltpu.VMEM((2, ROWS, PLANE), jnp.float32), spec, work,
            pltpu.VMEM((3, ROWS, PLANE), jnp.float32),
        ],
    )
    for share in (
        lax.ppermute(beside, "grid", swap),
        lax.ppermute(same, axes, home(False)),
        lax.ppermute(cross, axes, home(True)),
    ):
        total = total + share.astype(jnp.float32)
    return -total[None]


def solution(mesh):
    in_specs = (P("band", "grid", None),)
    out_specs = P("band", "grid", None)
    return jax.shard_map(
        on_device, mesh=mesh, in_specs=in_specs, out_specs=out_specs, check_vma=False
    )
```

profile of v0, /device:TPU:1, one launch (start us, length us, event | category | flops | bytes accessed | tf_op | source)
XLA Modules:
  0.0 51.9 jit_solution(14071297211350326992)
XLA Ops:
  0.0 0.0 copy-start
  0.0 1.0 %copy-done = f32[1,32,4096]{2,1,0:T(8,128)S(1)} copy-done((f32[1,32,4096]{2,1,0:T(8,128)S(1)}, f32[1,32,4096]{2,1,0:T(8,128)}, u32[]{:S(2)}) %copy-start) | copy-done | bytes 524312
  1.0 0.0 copy-start.1
  1.0 0.1 shard_map.55
  1.2 0.0 copy-start.4
  1.2 0.0 copy-start.5
  1.2 0.0 copy-start.6
  1.3 4.1 %collective-permute-start = (bf16[32,4224]{1,0:T(8,128)(2,1)S(1)}, bf16[32,4224]{1,0:T(8,128)(2,1)S(1)}, u32[]{:S(2)}, u32[]{:S(2)}) collective-permute-start(bf16[32,4224]{1,0:T(8,128)(2,1)S(1)} %shard_map.56.mine_ref), channel_id=1, source_target_pairs={{0,1},{1,0},{2,3},{3,2},{4,5},{5,4},{6,7},{7,6},{8,9},{9,8},{10,11... | collective-permute-start | bytes 811016 | tf_op jit(solution)/shard_map/ppermute | solution.py:261
  5.3 4.0 %collective-permute-start.2 = (bf16[32,4096]{1,0:T(8,128)(2,1)S(1)}, bf16[32,4096]{1,0:T(8,128)(2,1)S(1)}, u32[]{:S(2)}, u32[]{:S(2)}) collective-permute-start(bf16[32,4096]{1,0:T(8,128)(2,1)S(1)} %get-tuple-element.15), channel_id=1, source_target_pairs={{511,0},{508,1},{1,2},{510,3},{3,4},{0,5},{5,6},{2,7},{7,8},{4,9},... | collective-permute-start | bytes 786440 | tf_op jit(solution)/shard_map/ppermute | solution.py:259
  9.3 5.1 %collective-permute-start.1 = (bf16[32,4096]{1,0:T(8,128)(2,1)S(1)}, bf16[32,4096]{1,0:T(8,128)(2,1)S(1)}, u32[]{:S(2)}, u32[]{:S(2)}) collective-permute-start(bf16[32,4096]{1,0:T(8,128)(2,1)S(1)} %get-tuple-element.15), channel_id=1, source_target_pairs={{510,0},{509,1},{0,2},{511,3},{2,4},{1,5},{4,6},{3,7},{6,8},{5,9},... | collective-permute-start | bytes 786440 | tf_op jit(solution)/shard_map/ppermute | solution.py:258
  14.5 0.0 collective-permute-done.beside_ref
  14.5 0.0 copy-done.1
  14.5 0.0 copy-done.4
  14.5 0.0 copy-done.5
  14.5 0.0 copy-done.6
  14.5 0.0 copy-start.2
  14.5 1.2 %copy-done.2 = f32[64,4096]{1,0:T(8,128)S(1)} copy-done((f32[64,4096]{1,0:T(8,128)S(1)}, f32[64,4096]{1,0:T(8,128)}, u32[]{:S(2)}) %copy-start.2) | copy-done | bytes 1048600
  15.7 0.0 copy-start.3
  15.7 2.0 %shard_map.57 = (f32[32,4096]{1,0:T(8,128)S(1)}, f32[32,4096]{1,0:T(8,128)S(1)}) custom-call(f32[1,32,4096]{2,1,0:T(8,128)S(1)} %copy-done.1, bf16[32,4224]{1,0:T(8,128)(2,1)S(1)} %shard_map.56.mine_ref, bf16[32,4224]{1,0:T(8,128)(2,1)S(1)} %collective-permute-done.beside_ref, bf16[256,256]{1,0:T(8,128)(2,1)S(1)} %copy-done.4, bf16[64,64]{1,0:T(8,128)(2,1)S(1)} %copy-done.6, ...), custom_call_target="tpu_custom_call" | custom-call | tf_op jit(solution)/shard_map/pallas_call | solution.py:222
  17.8 1.0 %collective-permute-done.2.cross_ref = bf16[32,4096]{1,0:T(8,128)(2,1)S(1)} collective-permute-done((bf16[32,4096]{1,0:T(8,128)(2,1)S(1)}, bf16[32,4096]{1,0:T(8,128)(2,1)S(1)}, u32[]{:S(2)}, u32[]{:S(2)}) %collective-permute-start.2) | collective-permute-done | bytes 262176 | tf_op jit(solution)/shard_map/ppermute | solution.py:259
  18.7 0.0 collective-permute-done.1.same_ref
  18.7 0.0 copy-done.3
  18.7 2.5 %shard_map.58 = (f32[32,4096]{1,0:T(8,128)S(1)}, bf16[32,4096]{1,0:T(8,128)(2,1)S(1)}, bf16[32,4096]{1,0:T(8,128)(2,1)S(1)}, bf16[32,4096]{1,0:T(8,128)(2,1)S(1)}) custom-call(f32[1,32,4096]{2,1,0:T(8,128)S(1)} %copy-done.1, f32[32,4096]{1,0:T(8,128)S(1)} %get-tuple-element.14.beside_ref, bf16[32,4096]{1,0:T(8,128)(2,1)S(1)} %collective-permute-done.1.same_ref, ...), custom_call_target="tpu_custom_call" | custom-call | tf_op jit(solution)/shard_map/pallas_call | solution.py:222
  21.3 15.4 %collective-permute-start.3 = (bf16[32,4096]{1,0:T(8,128)(2,1)S(1)}, bf16[32,4096]{1,0:T(8,128)(2,1)S(1)}, u32[]{:S(2)}, u32[]{:S(2)}) collective-permute-start(bf16[32,4096]{1,0:T(8,128)(2,1)S(1)} %get-tuple-element.18), channel_id=1, source_target_pairs={{0,1},{1,0},{2,3},{3,2},{4,5},{5,4},{6,7},{7,6},{8,9},{9,8},{10,11... | collective-permute-start | bytes 786440 | tf_op jit(solution)/shard_map/ppermute | solution.py:274
  36.7 3.5 %collective-permute-start.4 = (bf16[32,4096]{1,0:T(8,128)(2,1)S(1)}, bf16[32,4096]{1,0:T(8,128)(2,1)S(1)}, u32[]{:S(2)}, u32[]{:S(2)}) collective-permute-start(bf16[32,4096]{1,0:T(8,128)(2,1)S(1)} %get-tuple-element.19), channel_id=1, source_target_pairs={{0,510},{1,509},{2,0},{3,511},{4,2},{5,1},{6,4},{7,3},{8,6},{9,5},... | collective-permute-start | bytes 786440 | tf_op jit(solution)/shard_map/ppermute | solution.py:275
  40.3 4.5 %collective-permute-start.5 = (bf16[32,4096]{1,0:T(8,128)(2,1)S(1)}, bf16[32,4096]{1,0:T(8,128)(2,1)S(1)}, u32[]{:S(2)}, u32[]{:S(2)}) collective-permute-start(bf16[32,4096]{1,0:T(8,128)(2,1)S(1)} %get-tuple-element.20), channel_id=1, source_target_pairs={{0,511},{1,508},{2,1},{3,510},{4,3},{5,0},{6,5},{7,2},{8,7},{9,4},... | collective-permute-start | bytes 786440 | tf_op jit(solution)/shard_map/ppermute | solution.py:276
  44.8 0.0 collective-permute-done.3
  44.8 0.0 collective-permute-done.4
  44.8 6.1 %collective-permute-done.5 = bf16[32,4096]{1,0:T(8,128)(2,1)S(1)} collective-permute-done((bf16[32,4096]{1,0:T(8,128)(2,1)S(1)}, bf16[32,4096]{1,0:T(8,128)(2,1)S(1)}, u32[]{:S(2)}, u32[]{:S(2)}) %collective-permute-start.5) | collective-permute-done | bytes 262176 | tf_op jit(solution)/shard_map/ppermute | solution.py:276
  50.9 0.9 %negate_bitcast_fusion = f32[1,32,4096]{2,1,0:T(8,128)} fusion(bf16[32,4096]{1,0:T(8,128)(2,1)S(1)} %collective-permute-done.5, bf16[32,4096]{1,0:T(8,128)(2,1)S(1)} %collective-permute-done.4, f32[32,4096]{1,0:T(8,128)S(1)} %get-tuple-element.17, bf16[32,4096]{1,0:T(8,128)(2,1)S(1)} %collective-permute-done.3), kind=kLoop, calls=%fused_computation | loop fusion | flops 917504 | bytes 1835008 | tf_op jit(solution)/shard_map/neg | solution.py:279
  (1 shorter events, 0.0 us)
Async XLA Ops:
  0.0 1.0 %copy-start = (f32[1,32,4096]{2,1,0:T(8,128)S(1)}, f32[1,32,4096]{2,1,0:T(8,128)}, u32[]{:S(2)}) copy-start(f32[1,32,4096]{2,1,0:T(8,128)} %psi_ref.5) | copy-start | bytes 1572868
  1.0 13.4 %copy-start.1 = (f32[1,32,4096]{2,1,0:T(8,128)S(1)}, f32[1,32,4096]{2,1,0:T(8,128)}, u32[]{:S(2)}) copy-start(f32[1,32,4096]{2,1,0:T(8,128)} %psi_ref.5) | copy-start | bytes 1572868
  1.2 13.3 %copy-start.4 = (bf16[256,256]{1,0:T(8,128)(2,1)S(1)}, bf16[256,256]{1,0:T(8,128)(2,1)}, u32[]{:S(2)}) copy-start(bf16[256,256]{1,0:T(8,128)(2,1)} %constant.13.plane_ref) | copy-start | bytes 393220
  1.2 13.3 %copy-start.5 = (bf16[64,192]{1,0:T(8,128)(2,1)S(1)}, bf16[64,192]{1,0:T(8,128)(2,1)}, u32[]{:S(2)}) copy-start(bf16[64,192]{1,0:T(8,128)(2,1)} %constant.10.clone.wide_ref) | copy-start | bytes 73732
  1.2 13.3 %copy-start.6 = (bf16[64,64]{1,0:T(8,128)(2,1)S(1)}, bf16[64,64]{1,0:T(8,128)(2,1)}, u32[]{:S(2)}) copy-start(bf16[64,64]{1,0:T(8,128)(2,1)} %constant.9.clone.low_ref) | copy-start | bytes 24580
  1.3 13.2 %collective-permute-start = (bf16[32,4224]{1,0:T(8,128)(2,1)S(1)}, bf16[32,4224]{1,0:T(8,128)(2,1)S(1)}, u32[]{:S(2)}, u32[]{:S(2)}) collective-permute-start(bf16[32,4224]{1,0:T(8,128)(2,1)S(1)} %shard_map.56.mine_ref), channel_id=1, source_target_pairs={{0,1},{1,0},{2,3},{3,2},{4,5},{5,4},{6,7},{7,6},{8,9},{9,8},{10,11... | collective-permute-start | bytes 811016 | tf_op jit(solution)/shard_map/ppermute | solution.py:261
  5.3 13.4 %collective-permute-start.2 = (bf16[32,4096]{1,0:T(8,128)(2,1)S(1)}, bf16[32,4096]{1,0:T(8,128)(2,1)S(1)}, u32[]{:S(2)}, u32[]{:S(2)}) collective-permute-start(bf16[32,4096]{1,0:T(8,128)(2,1)S(1)} %get-tuple-element.15), channel_id=1, source_target_pairs={{511,0},{508,1},{1,2},{510,3},{3,4},{0,5},{5,6},{2,7},{7,8},{4,9},... | collective-permute-start | bytes 786440 | tf_op jit(solution)/shard_map/ppermute | solution.py:259
  9.3 9.4 %collective-permute-start.1 = (bf16[32,4096]{1,0:T(8,128)(2,1)S(1)}, bf16[32,4096]{1,0:T(8,128)(2,1)S(1)}, u32[]{:S(2)}, u32[]{:S(2)}) collective-permute-start(bf16[32,4096]{1,0:T(8,128)(2,1)S(1)} %get-tuple-element.15), channel_id=1, source_target_pairs={{510,0},{509,1},{0,2},{511,3},{2,4},{1,5},{4,6},{3,7},{6,8},{5,9},... | collective-permute-start | bytes 786440 | tf_op jit(solution)/shard_map/ppermute | solution.py:258
  14.5 1.2 %copy-start.2 = (f32[64,4096]{1,0:T(8,128)S(1)}, f32[64,4096]{1,0:T(8,128)}, u32[]{:S(2)}) copy-start(f32[64,4096]{1,0:T(8,128)} %constant.11.clone.table_ref) | copy-start | bytes 3145732
  15.7 3.0 %copy-start.3 = (f32[64,4096]{1,0:T(8,128)S(1)}, f32[64,4096]{1,0:T(8,128)}, u32[]{:S(2)}) copy-start(f32[64,4096]{1,0:T(8,128)} %constant.11.clone.table_ref) | copy-start | bytes 3145732
  21.3 23.6 %collective-permute-start.3 = (bf16[32,4096]{1,0:T(8,128)(2,1)S(1)}, bf16[32,4096]{1,0:T(8,128)(2,1)S(1)}, u32[]{:S(2)}, u32[]{:S(2)}) collective-permute-start(bf16[32,4096]{1,0:T(8,128)(2,1)S(1)} %get-tuple-element.18), channel_id=1, source_target_pairs={{0,1},{1,0},{2,3},{3,2},{4,5},{5,4},{6,7},{7,6},{8,9},{9,8},{10,11... | collective-permute-start | bytes 786440 | tf_op jit(solution)/shard_map/ppermute | solution.py:274
  36.7 8.1 %collective-permute-start.4 = (bf16[32,4096]{1,0:T(8,128)(2,1)S(1)}, bf16[32,4096]{1,0:T(8,128)(2,1)S(1)}, u32[]{:S(2)}, u32[]{:S(2)}) collective-permute-start(bf16[32,4096]{1,0:T(8,128)(2,1)S(1)} %get-tuple-element.19), channel_id=1, source_target_pairs={{0,510},{1,509},{2,0},{3,511},{4,2},{5,1},{6,4},{7,3},{8,6},{9,5},... | collective-permute-start | bytes 786440 | tf_op jit(solution)/shard_map/ppermute | solution.py:275
  40.3 10.7 %collective-permute-start.5 = (bf16[32,4096]{1,0:T(8,128)(2,1)S(1)}, bf16[32,4096]{1,0:T(8,128)(2,1)S(1)}, u32[]{:S(2)}, u32[]{:S(2)}) collective-permute-start(bf16[32,4096]{1,0:T(8,128)(2,1)S(1)} %get-tuple-element.20), channel_id=1, source_target_pairs={{0,511},{1,508},{2,1},{3,510},{4,3},{5,0},{6,5},{7,2},{8,7},{9,4},... | collective-permute-start | bytes 786440 | tf_op jit(solution)/shard_map/ppermute | solution.py:276
where the time goes:
time: 52.2 us; the launch traced here: 51.9 us
  starting transfers between devices  36.7 us (70%)
  waiting for transfers between devices  7.1 us (14%)
  Pallas kernels  4.67 us (9%)
  local copies, waits for them, and re-layouts  2.32 us (4%)
  other arithmetic  0.92 us (2%)
    ppermute x1, starting transfers between devices, on_device(): lax.ppermute(beside, 'grid', swap)  15.4 us
    ppermute x1, waiting for transfers between devices, on_device(): lax.ppermute(cross, axes, home(True))  6.1 us
    ppermute x1, starting transfers between devices, on_device(): same = lax.ppermute(code, axes, route(False))  5.12 us
    pallas_call x4, Pallas kernels, call(): pl.pallas_call(kernel, out_shape=outs, in_specs=[vmem] * len(args), out_s...  4.67 us
    ppermute x1, starting transfers between devices, on_device(): lax.ppermute(cross, axes, home(True))  4.55 us
    ppermute x1, starting transfers between devices, on_device(): beside = lax.ppermute(marked, 'grid', swap)  4.08 us
    ppermute x1, starting transfers between devices, on_device(): cross = lax.ppermute(code, axes, route(True))  3.97 us
    ppermute x1, starting transfers between devices, on_device(): lax.ppermute(same, axes, home(False))  3.54 us
  transfers between devices with their start and end apart: 6, of which 2 were waited for; matrix products, arithmetic and copies ran while one was open for 0% of the time, Pallas kernels for 4%

commit v1 on v0

--- a/solution.py
+++ b/solution.py
@@ -45,17 +45,14 @@
     return high, np.concatenate([high, high, low], axis=1)
 
 
-def kernel_table():
+def column_squares():
     count = np.arange(NG)
     folded = np.where(count < NG // 2, count, count - NG)
-    square = (folded * folded).astype(np.float64)
+    square = (folded * folded).astype(np.float32)
     block, upper, last = np.meshgrid(
         np.arange(BLOCKS), np.arange(2), np.arange(NG), indexing="ij"
     )
-    column = (square[block + BLOCKS * upper] + square[last]).reshape(1, PLANE)
-    msq = square[:, None] + column
-    table = np.where(msq > 0.0, coulomb / np.maximum(msq, 1.0), 0.0) / NG**3
-    return table.astype(np.float32)
+    return (square[block + BLOCKS * upper] + square[last]).reshape(1, PLANE)
 
 
 def hartley(items):
@@ -141,11 +138,16 @@
             spec_ref[:, lane_block(first + b)] = spec[b * NG : (b + 1) * NG]
 
 
-def screen(spec_ref, low_ref, wide_ref, table_ref, rows):
+def screen(spec_ref, low_ref, wide_ref, column_ref, rows):
+    count = lax.broadcasted_iota(jnp.int32, (NG, WIDTH), 0)
+    folded = jnp.where(count < NG // 2, count, count - NG)
+    square = (folded * folded).astype(jnp.float32)
     for first in range(0, PLANE, WIDTH):
         lanes = slice(first, first + WIDTH)
+        msq = square + column_ref[:, lanes]
+        scaled = (coulomb / NG**3) / jnp.maximum(msq, 1.0)
         value = jnp.dot(low_ref[...], spec_ref[:, lanes], preferred_element_type=jnp.float32)
-        value = value * table_ref[:, lanes]
+        value = value * jnp.where(msq > 0.0, scaled, 0.0)
         high = value.astype(jnp.bfloat16)
         low = (value - high.astype(jnp.float32)).astype(jnp.bfloat16)
         operand = jnp.concatenate([high, low, high], axis=0)
@@ -171,35 +173,20 @@
     out_ref[...] = code_ref[...]
 
 
-def self_kernel(psi_ref, mine_ref, beside_ref, plane_ref, low_ref, wide_ref, table_ref,
-                beside_out, total_out, spec, scratch):
-    beside_out[...] = decoded(beside_ref[:, :PLANE])
-    band = (psi_ref.at[0], beside_out)
-    forward(band, band, plane_ref, spec, scratch)
-    first = lax.broadcasted_iota(jnp.int32, (ROWS, LANES), 1) == 0
-    for rows, ref in ((slice(0, ROWS), mine_ref), (slice(ROWS, NG), beside_ref)):
-        spec[rows, :LANES] = jnp.where(first, ref[:, PLANE:], spec[rows, :LANES])
-    screen(spec, low_ref, wide_ref, table_ref, ROWS)
-
-    def use(slab, rows, lanes, item):
-        total_out[rows, lanes] = psi_ref[0, rows, lanes] * item
-
-    inverse(spec, plane_ref, scratch, ROWS, use)
-
-
-def pair_kernel(psi_ref, beside_ref, same_ref, cross_ref, plane_ref, low_ref, wide_ref,
-                table_ref, part_ref, total_out, beside_out, same_out, cross_out,
+def pair_kernel(cross_ref, same_ref, beside_code, psi_ref, plane_ref, low_ref, wide_ref,
+                column_ref, part_out, field_out, beside_out, same_out, cross_out,
                 other, spec, scratch, sums):
     other[0] = decoded(same_ref[...])
     other[1] = decoded(cross_ref[...])
-    band = (psi_ref.at[0], beside_ref)
+    field_out[...] = decoded(beside_code[:, :PLANE])
+    band = (psi_ref.at[0], field_out)
     forward(band, (other.at[0], other.at[1]), plane_ref, spec, scratch)
-    screen(spec, low_ref, wide_ref, table_ref, NG)
+    screen(spec, low_ref, wide_ref, column_ref, NG)
 
     def use(slab, rows, lanes, item):
         part = other[slab, rows, lanes] * item
         if slab == 0:
-            total_out[rows, lanes] = part_ref[rows, lanes] + part
+            part_out[rows, lanes] = part
         else:
             sums[2, rows, lanes] = part
         sums[slab, rows, lanes] = band[slab][rows, lanes] * item
@@ -210,8 +197,23 @@
     beside_out[...] = sums[2].astype(jnp.bfloat16)
 
 
+def self_kernel(psi_ref, mine_ref, beside_code, field_ref, plane_ref, low_ref, wide_ref,
+                column_ref, part_ref, total_out, spec, scratch):
+    band = (psi_ref.at[0], field_ref)
+    forward(band, band, plane_ref, spec, scratch)
+    first = lax.broadcasted_iota(jnp.int32, (ROWS, LANES), 1) == 0
+    for rows, ref in ((slice(0, ROWS), mine_ref), (slice(ROWS, NG), beside_code)):
+        spec[rows, :LANES] = jnp.where(first, ref[:, PLANE:], spec[rows, :LANES])
+    screen(spec, low_ref, wide_ref, column_ref, ROWS)
+
+    def use(slab, rows, lanes, item):
+        total_out[rows, lanes] = part_ref[rows, lanes] + psi_ref[0, rows, lanes] * item
+
+    inverse(spec, plane_ref, scratch, ROWS, use)
+
+
 vmem = pl.BlockSpec(memory_space=pltpu.VMEM)
-limit = pltpu.CompilerParams(vmem_limit_bytes=40 * 1024 * 1024)
+limit = pltpu.CompilerParams(vmem_limit_bytes=14 * 1024 * 1024)
 
 
 def shape(dims, dtype):
@@ -245,8 +247,8 @@
     plane = jnp.asarray(plane_matrix())
     stacked = jnp.concatenate([plane, plane], axis=0)
     x_low, x_wide = (jnp.asarray(m) for m in x_matrices())
-    table = jnp.asarray(kernel_table())
-    tables = (stacked, x_low, x_wide, table)
+    column = jnp.asarray(column_squares())
+    tables = (stacked, x_low, x_wide, column)
 
     sent = shape((ROWS, PLANE), jnp.bfloat16)
     field = shape((ROWS, PLANE), jnp.float32)
@@ -259,21 +261,22 @@
     cross = lax.ppermute(code, axes, route(True))
     marked = call(copy_kernel, marks, marked)
     beside = lax.ppermute(marked, "grid", swap)
-    beside, total = call(
-        self_kernel, (field, field), orbitals, marked, beside, *tables, scratch=[spec, work]
-    )
-    total, beside, same, cross = call(
-        pair_kernel, (field, sent, sent, sent),
-        orbitals, beside, same, cross, *tables, total,
+    part, partner, beside_share, same, cross = call(
+        pair_kernel, (field, field, sent, sent, sent),
+        cross, same, beside, orbitals, *tables,
         scratch=[
             pltpu.VMEM((2, ROWS, PLANE), jnp.float32), spec, work,
             pltpu.VMEM((3, ROWS, PLANE), jnp.float32),
         ],
     )
+    total = call(
+        self_kernel, field, orbitals, marked, beside, partner, *tables, part,
+        scratch=[spec, work],
+    )
     for share in (
-        lax.ppermute(beside, "grid", swap),
+        lax.ppermute(cross, axes, home(True)),
         lax.ppermute(same, axes, home(False)),
-        lax.ppermute(cross, axes, home(True)),
+        lax.ppermute(beside_share, "grid", swap),
     ):
         total = total + share.astype(jnp.float32)
     return -total[None]

time: 52.2 us -> 51.3 us (0.983)
  waiting for transfers between devices: 7.1 us -> 17.3 us
  starting transfers between devices: 36.7 us -> 26.9 us
  local copies, waits for them, and re-layouts: 2.32 us -> 1.11 us
    ppermute x1, starting transfers between devices: 15.4 us -> 2.53 us  [on_device(): lax.ppermute(beside_share, 'grid', swap)]
    ppermute x1, waiting for transfers between devices: 0.99 us -> 11.8 us  [on_device(): cross = lax.ppermute(code, axes, route(True))]
    ppermute x1, waiting for transfers between devices: 6.1 us -> 0.05 us  [on_device(): lax.ppermute(cross, axes, home(True))]
    ppermute x1, starting transfers between devices: 4.55 us -> 10.4 us  [on_device(): lax.ppermute(cross, axes, home(True))]
    ppermute x1, waiting for transfers between devices: 0.01 us -> 4.03 us  [on_device(): lax.ppermute(beside_share, 'grid', swap)]
    ppermute x1, starting transfers between devices: 3.54 us -> 1.92 us  [on_device(): lax.ppermute(same, axes, home(False))]
    unnamed x14 -> x12, local copies, waits for them, and re-layouts: 2.32 us -> 1.11 us
    ppermute x1, waiting for transfers between devices: 0.01 us -> 1.19 us  [on_device(): lax.ppermute(same, axes, home(False))]
  transfers between devices with their start and end apart: 6 -> 6, of which waited for: 2 -> 5; matrix products, arithmetic and copies ran while one was open for 0% -> 0% of each run, Pallas kernels for 4% -> 4%
where the time goes in v1:
time: 51.3 us; the launch traced here: 51 us
  starting transfers between devices  26.9 us (52%)
  waiting for transfers between devices  17.3 us (34%)
  Pallas kernels  4.74 us (9%)
  local copies, waits for them, and re-layouts  1.11 us (2%)
  other arithmetic  0.92 us (2%)
    ppermute x1, waiting for transfers between devices, on_device(): cross = lax.ppermute(code, axes, route(True))  11.8 us
    ppermute x1, starting transfers between devices, on_device(): lax.ppermute(cross, axes, home(True))  10.4 us
    ppermute x1, starting transfers between devices, on_device(): same = lax.ppermute(code, axes, route(False))  4.84 us
    pallas_call x4, Pallas kernels, call(): pl.pallas_call(kernel, out_shape=outs, in_specs=[vmem] * len(args), out_s...  4.74 us
    ppermute x1, starting transfers between devices, on_device(): beside = lax.ppermute(marked, 'grid', swap)  4.08 us
    ppermute x1, waiting for transfers between devices, on_device(): lax.ppermute(beside_share, 'grid', swap)  4.03 us
    ppermute x1, starting transfers between devices, on_device(): cross = lax.ppermute(code, axes, route(True))  3.13 us
    ppermute x1, starting transfers between devices, on_device(): lax.ppermute(beside_share, 'grid', swap)  2.53 us
  transfers between devices with their start and end apart: 6, of which 5 were waited for; matrix products, arithmetic and copies ran while one was open for 0% of the time, Pallas kernels for 4%

profile of v1, /device:TPU:1, one launch (start us, length us, event | category | flops | bytes accessed | tf_op | source)
XLA Modules:
  0.0 51.0 jit_solution(15087844118439150765)
XLA Ops:
  0.0 0.0 copy-start
  0.0 1.0 %copy-done = f32[1,32,4096]{2,1,0:T(8,128)S(1)} copy-done((f32[1,32,4096]{2,1,0:T(8,128)S(1)}, f32[1,32,4096]{2,1,0:T(8,128)}, u32[]{:S(2)}) %copy-start) | copy-done | bytes 524312
  1.0 0.0 copy-start.1
  1.0 0.1 shard_map.55
  1.2 0.0 copy-start.2
  1.2 0.0 copy-start.3
  1.2 0.0 copy-start.4
  1.2 0.0 copy-start.5
  1.3 4.1 %collective-permute-start = (bf16[32,4224]{1,0:T(8,128)(2,1)S(1)}, bf16[32,4224]{1,0:T(8,128)(2,1)S(1)}, u32[]{:S(2)}, u32[]{:S(2)}) collective-permute-start(bf16[32,4224]{1,0:T(8,128)(2,1)S(1)} %shard_map.56.mine_ref), channel_id=1, source_target_pairs={{0,1},{1,0},{2,3},{3,2},{4,5},{5,4},{6,7},{7,6},{8,9},{9,8},{10,11... | collective-permute-start | bytes 811016 | tf_op jit(solution)/shard_map/ppermute | solution.py:263
  5.4 4.8 %collective-permute-start.2 = (bf16[32,4096]{1,0:T(8,128)(2,1)S(1)}, bf16[32,4096]{1,0:T(8,128)(2,1)S(1)}, u32[]{:S(2)}, u32[]{:S(2)}) collective-permute-start(bf16[32,4096]{1,0:T(8,128)(2,1)S(1)} %get-tuple-element.13), channel_id=1, source_target_pairs={{510,0},{509,1},{0,2},{511,3},{2,4},{1,5},{4,6},{3,7},{6,8},{5,9},... | collective-permute-start | bytes 786440 | tf_op jit(solution)/shard_map/ppermute | solution.py:260
  10.2 3.1 %collective-permute-start.1 = (bf16[32,4096]{1,0:T(8,128)(2,1)S(1)}, bf16[32,4096]{1,0:T(8,128)(2,1)S(1)}, u32[]{:S(2)}, u32[]{:S(2)}) collective-permute-start(bf16[32,4096]{1,0:T(8,128)(2,1)S(1)} %get-tuple-element.13), channel_id=1, source_target_pairs={{511,0},{508,1},{1,2},{510,3},{3,4},{0,5},{5,6},{2,7},{7,8},{4,9},... | collective-permute-start | bytes 786440 | tf_op jit(solution)/shard_map/ppermute | solution.py:261
  13.3 0.2 collective-permute-done.2.same_ref
  13.5 11.8 %collective-permute-done.1.cross_ref = bf16[32,4096]{1,0:T(8,128)(2,1)S(1)} collective-permute-done((bf16[32,4096]{1,0:T(8,128)(2,1)S(1)}, bf16[32,4096]{1,0:T(8,128)(2,1)S(1)}, u32[]{:S(2)}, u32[]{:S(2)}) %collective-permute-start.1) | collective-permute-done | bytes 262176 | tf_op jit(solution)/shard_map/ppermute | solution.py:261
  25.3 0.0 collective-permute-done.beside_code
  25.3 0.0 copy-done.1
  25.3 0.0 copy-done.2
  25.3 0.0 copy-done.3
  25.4 0.0 copy-done.4
  25.4 0.0 copy-done.5
  25.4 2.6 %shard_map.57 = (f32[32,4096]{1,0:T(8,128)S(1)}, f32[32,4096]{1,0:T(8,128)S(1)}, bf16[32,4096]{1,0:T(8,128)(2,1)S(1)}, bf16[32,4096]{1,0:T(8,128)(2,1)S(1)}, bf16[32,4096]{1,0:T(8,128)(2,1)S(1)}) custom-call(bf16[32,4096]{1,0:T(8,128)(2,1)S(1)} %collective-permute-done.1.cross_ref, bf16[32,4096]{1,0:T(8,128)(2,1)S(1)} %collective-permute-done.2.same_ref, ...), custom_call_target="tpu_custom_call" | custom-call | tf_op jit(solution)/shard_map/pallas_call | solution.py:224
  28.0 10.4 %collective-permute-start.3 = (bf16[32,4096]{1,0:T(8,128)(2,1)S(1)}, bf16[32,4096]{1,0:T(8,128)(2,1)S(1)}, u32[]{:S(2)}, u32[]{:S(2)}) collective-permute-start(bf16[32,4096]{1,0:T(8,128)(2,1)S(1)} %get-tuple-element.16), channel_id=1, source_target_pairs={{0,511},{1,508},{2,1},{3,510},{4,3},{5,0},{6,5},{7,2},{8,7},{9,4},... | collective-permute-start | bytes 786440 | tf_op jit(solution)/shard_map/ppermute | solution.py:277
  38.4 1.9 %collective-permute-start.4 = (bf16[32,4096]{1,0:T(8,128)(2,1)S(1)}, bf16[32,4096]{1,0:T(8,128)(2,1)S(1)}, u32[]{:S(2)}, u32[]{:S(2)}) collective-permute-start(bf16[32,4096]{1,0:T(8,128)(2,1)S(1)} %get-tuple-element.17), channel_id=1, source_target_pairs={{0,510},{1,509},{2,0},{3,511},{4,2},{5,1},{6,4},{7,3},{8,6},{9,5},... | collective-permute-start | bytes 786440 | tf_op jit(solution)/shard_map/ppermute | solution.py:278
  40.3 2.5 %collective-permute-start.5 = (bf16[32,4096]{1,0:T(8,128)(2,1)S(1)}, bf16[32,4096]{1,0:T(8,128)(2,1)S(1)}, u32[]{:S(2)}, u32[]{:S(2)}) collective-permute-start(bf16[32,4096]{1,0:T(8,128)(2,1)S(1)} %get-tuple-element.18), channel_id=1, source_target_pairs={{0,1},{1,0},{2,3},{3,2},{4,5},{5,4},{6,7},{7,6},{8,9},{9,8},{10,11... | collective-permute-start | bytes 786440 | tf_op jit(solution)/shard_map/ppermute | solution.py:279
  42.9 2.0 %shard_map.58 = f32[32,4096]{1,0:T(8,128)S(1)} custom-call(f32[1,32,4096]{2,1,0:T(8,128)S(1)} %copy-done.1, bf16[32,4224]{1,0:T(8,128)(2,1)S(1)} %shard_map.56.mine_ref, bf16[32,4224]{1,0:T(8,128)(2,1)S(1)} %collective-permute-done.beside_code, f32[32,4096]{1,0:T(8,128)S(1)} %get-tuple-element.14.field_ref, bf16[256,256]{1,0:T(8,128)(2,1)S(1)} %copy-done.2, ...), custom_call_target="tpu_custom_call" | custom-call | tf_op jit(solution)/shard_map/pallas_call | solution.py:224
  44.8 0.1 collective-permute-done.3
  44.9 1.2 %collective-permute-done.4 = bf16[32,4096]{1,0:T(8,128)(2,1)S(1)} collective-permute-done((bf16[32,4096]{1,0:T(8,128)(2,1)S(1)}, bf16[32,4096]{1,0:T(8,128)(2,1)S(1)}, u32[]{:S(2)}, u32[]{:S(2)}) %collective-permute-start.4) | collective-permute-done | bytes 262176 | tf_op jit(solution)/shard_map/ppermute | solution.py:278
  46.1 4.0 %collective-permute-done.5 = bf16[32,4096]{1,0:T(8,128)(2,1)S(1)} collective-permute-done((bf16[32,4096]{1,0:T(8,128)(2,1)S(1)}, bf16[32,4096]{1,0:T(8,128)(2,1)S(1)}, u32[]{:S(2)}, u32[]{:S(2)}) %collective-permute-start.5) | collective-permute-done | bytes 262176 | tf_op jit(solution)/shard_map/ppermute | solution.py:279
  50.1 0.9 %negate_bitcast_fusion = f32[1,32,4096]{2,1,0:T(8,128)} fusion(bf16[32,4096]{1,0:T(8,128)(2,1)S(1)} %collective-permute-done.5, bf16[32,4096]{1,0:T(8,128)(2,1)S(1)} %collective-permute-done.4, f32[32,4096]{1,0:T(8,128)S(1)} %shard_map.58, bf16[32,4096]{1,0:T(8,128)(2,1)S(1)} %collective-permute-done.3), kind=kLoop, calls=%fused_computation | loop fusion | flops 917504 | bytes 1835008 | tf_op jit(solution)/shard_map/neg | solution.py:282
  (1 shorter events, 0.0 us)
Async XLA Ops:
  0.0 1.0 %copy-start = (f32[1,32,4096]{2,1,0:T(8,128)S(1)}, f32[1,32,4096]{2,1,0:T(8,128)}, u32[]{:S(2)}) copy-start(f32[1,32,4096]{2,1,0:T(8,128)} %psi_ref.5) | copy-start | bytes 1572868
  1.0 24.3 %copy-start.1 = (f32[1,32,4096]{2,1,0:T(8,128)S(1)}, f32[1,32,4096]{2,1,0:T(8,128)}, u32[]{:S(2)}) copy-start(f32[1,32,4096]{2,1,0:T(8,128)} %psi_ref.5) | copy-start | bytes 1572868
  1.2 24.2 %copy-start.2 = (bf16[256,256]{1,0:T(8,128)(2,1)S(1)}, bf16[256,256]{1,0:T(8,128)(2,1)}, u32[]{:S(2)}) copy-start(bf16[256,256]{1,0:T(8,128)(2,1)} %constant.13.plane_ref) | copy-start | bytes 393220
  1.2 24.2 %copy-start.3 = (bf16[64,192]{1,0:T(8,128)(2,1)S(1)}, bf16[64,192]{1,0:T(8,128)(2,1)}, u32[]{:S(2)}) copy-start(bf16[64,192]{1,0:T(8,128)(2,1)} %constant.10.clone.wide_ref) | copy-start | bytes 73732
  1.2 24.1 %copy-start.4 = (f32[1,4096]{1,0:T(1,128)S(1)}, f32[1,4096]{1,0:T(1,128)}, u32[]{:S(2)}) copy-start(f32[1,4096]{1,0:T(1,128)} %constant.11.clone.column_ref) | copy-start | bytes 49156
  1.2 24.1 %copy-start.5 = (bf16[64,64]{1,0:T(8,128)(2,1)S(1)}, bf16[64,64]{1,0:T(8,128)(2,1)}, u32[]{:S(2)}) copy-start(bf16[64,64]{1,0:T(8,128)(2,1)} %constant.9.clone.low_ref) | copy-start | bytes 24580
  1.3 24.1 %collective-permute-start = (bf16[32,4224]{1,0:T(8,128)(2,1)S(1)}, bf16[32,4224]{1,0:T(8,128)(2,1)S(1)}, u32[]{:S(2)}, u32[]{:S(2)}) collective-permute-start(bf16[32,4224]{1,0:T(8,128)(2,1)S(1)} %shard_map.56.mine_ref), channel_id=1, source_target_pairs={{0,1},{1,0},{2,3},{3,2},{4,5},{5,4},{6,7},{7,6},{8,9},{9,8},{10,11... | collective-permute-start | bytes 811016 | tf_op jit(solution)/shard_map/ppermute | solution.py:263
  5.4 8.1 %collective-permute-start.2 = (bf16[32,4096]{1,0:T(8,128)(2,1)S(1)}, bf16[32,4096]{1,0:T(8,128)(2,1)S(1)}, u32[]{:S(2)}, u32[]{:S(2)}) collective-permute-start(bf16[32,4096]{1,0:T(8,128)(2,1)S(1)} %get-tuple-element.13), channel_id=1, source_target_pairs={{510,0},{509,1},{0,2},{511,3},{2,4},{1,5},{4,6},{3,7},{6,8},{5,9},... | collective-permute-start | bytes 786440 | tf_op jit(solution)/shard_map/ppermute | solution.py:260
  10.2 15.1 %collective-permute-start.1 = (bf16[32,4096]{1,0:T(8,128)(2,1)S(1)}, bf16[32,4096]{1,0:T(8,128)(2,1)S(1)}, u32[]{:S(2)}, u32[]{:S(2)}) collective-permute-start(bf16[32,4096]{1,0:T(8,128)(2,1)S(1)} %get-tuple-element.13), channel_id=1, source_target_pairs={{511,0},{508,1},{1,2},{510,3},{3,4},{0,5},{5,6},{2,7},{7,8},{4,9},... | collective-permute-start | bytes 786440 | tf_op jit(solution)/shard_map/ppermute | solution.py:261
  28.0 16.9 %collective-permute-start.3 = (bf16[32,4096]{1,0:T(8,128)(2,1)S(1)}, bf16[32,4096]{1,0:T(8,128)(2,1)S(1)}, u32[]{:S(2)}, u32[]{:S(2)}) collective-permute-start(bf16[32,4096]{1,0:T(8,128)(2,1)S(1)} %get-tuple-element.16), channel_id=1, source_target_pairs={{0,511},{1,508},{2,1},{3,510},{4,3},{5,0},{6,5},{7,2},{8,7},{9,4},... | collective-permute-start | bytes 786440 | tf_op jit(solution)/shard_map/ppermute | solution.py:277
  38.4 7.7 %collective-permute-start.4 = (bf16[32,4096]{1,0:T(8,128)(2,1)S(1)}, bf16[32,4096]{1,0:T(8,128)(2,1)S(1)}, u32[]{:S(2)}, u32[]{:S(2)}) collective-permute-start(bf16[32,4096]{1,0:T(8,128)(2,1)S(1)} %get-tuple-element.17), channel_id=1, source_target_pairs={{0,510},{1,509},{2,0},{3,511},{4,2},{5,1},{6,4},{7,3},{8,6},{9,5},... | collective-permute-start | bytes 786440 | tf_op jit(solution)/shard_map/ppermute | solution.py:278
  40.3 9.8 %collective-permute-start.5 = (bf16[32,4096]{1,0:T(8,128)(2,1)S(1)}, bf16[32,4096]{1,0:T(8,128)(2,1)S(1)}, u32[]{:S(2)}, u32[]{:S(2)}) collective-permute-start(bf16[32,4096]{1,0:T(8,128)(2,1)S(1)} %get-tuple-element.18), channel_id=1, source_target_pairs={{0,1},{1,0},{2,3},{3,2},{4,5},{5,4},{6,7},{7,6},{8,9},{9,8},{10,11... | collective-permute-start | bytes 786440 | tf_op jit(solution)/shard_map/ppermute | solution.py:279

commit v2 on v1

--- a/solution.py
+++ b/solution.py
@@ -94,48 +94,53 @@
     return slice(b * LANES, (b + 1) * LANES)
 
 
-def pairwise(items):
-    while len(items) > 1:
-        items = [a + b for a, b in zip(items[0::2], items[1::2])]
-    return items[0]
-
-
-def pairwise(items):
-    while len(items) > 1:
-        items = [a + b for a, b in zip(items[0::2], items[1::2])]
-    return items[0]
-
-
-def encode_kernel(psi_ref, code_ref, marked_ref):
-    psi = psi_ref[0]
-    code = jnp.exp2(psi * CODE).astype(jnp.bfloat16)
+def encode_kernel(psi_ref, code_ref, wide_ref):
+    code = jnp.exp2(psi_ref[0] * CODE).astype(jnp.bfloat16)
     code_ref[...] = code
-    marked_ref[:, :PLANE] = code
-    part = pairwise([psi[:, lane_block(b)] ** 2 for b in range(BLOCKS)])
-    coarse = jnp.round(part * 512.0) * (1.0 / 512.0)
-    total = jnp.sum(coarse, axis=1, keepdims=True) + jnp.sum(part - coarse, axis=1, keepdims=True)
-    marked_ref[:, PLANE:] = jnp.broadcast_to(total, (ROWS, LANES)).astype(jnp.bfloat16)
-
-
-def forward(mine, other, plane_ref, spec_ref, scratch):
-    for tile in range(NG // 8):
-        slab, row = divmod(8 * tile, ROWS)
-        rows = slice(row, row + 8)
-        fields = [
-            mine[slab][rows, lane_block(b)] * other[slab][rows, lane_block(b)]
-            for b in range(BLOCKS)
-        ]
+    wide_ref[:, :PLANE] = code
+    wide_ref[:, PLANE:] = jnp.zeros((ROWS, 2 * LANES), jnp.bfloat16)
+
+
+def mark_kernel(psi_ref, code_ref, marked_ref, turned):
+    group = LANES // ROWS
+    for t in range(BLOCKS // group):
+        squares = [psi_ref[0, :, lane_block(t * group + k)] ** 2 for k in range(group)]
+        turned[t * LANES : (t + 1) * LANES, :] = jnp.concatenate(squares, axis=0).T
+    chains = 2 * BLOCKS // group
+    along_z = turned[pl.ds(0, chains, stride=NG), :]
+    for z in range(1, NG):
+        along_z = along_z + turned[pl.ds(z, chains, stride=NG), :]
+    shifted = [along_z] + [
+        pltpu.roll(along_z, LANES - k * ROWS, axis=1) for k in range(1, group)
+    ]
+    total = None
+    for t in range(BLOCKS // group):
+        for k in range(group):
+            for e in range(2):
+                row = shifted[k][2 * t + e : 2 * t + e + 1]
+                total = row if total is None else total + row
+    marked_ref[:, :PLANE] = code_ref[...]
+    column = jnp.broadcast_to(total, (LANES, LANES)).T[:ROWS]
+    marked_ref[:, PLANE:] = column.astype(jnp.bfloat16)
+
+
+def forward(mine, other, plane_ref, spec_ref, first_row, scratch):
+    for tile in range(ROWS // 8):
+        rows = slice(8 * tile, 8 * tile + 8)
+        fields = [mine[rows, lane_block(b)] * other[rows, lane_block(b)] for b in range(BLOCKS)]
         for b, item in enumerate(twist(hartley(fields))):
-            scratch[b * NG + 8 * tile : b * NG + 8 * tile + 8, :] = item
+            scratch[b * ROWS + 8 * tile : b * ROWS + 8 * tile + 8, :] = item
     for first in range(0, BLOCKS, CHUNK):
-        value = scratch[first * NG : (first + CHUNK) * NG, :]
+        value = scratch[first * ROWS : (first + CHUNK) * ROWS, :]
         high = value.astype(jnp.bfloat16)
         low = (value - high.astype(jnp.float32)).astype(jnp.bfloat16)
         operand = jnp.concatenate([high, low], axis=1)
         both = jnp.dot(operand, plane_ref[...], preferred_element_type=jnp.float32)
         spec = (both[:, :LANES] + both[:, LANES:]).astype(jnp.bfloat16)
         for b in range(CHUNK):
-            spec_ref[:, lane_block(first + b)] = spec[b * NG : (b + 1) * NG]
+            spec_ref[first_row : first_row + ROWS, lane_block(first + b)] = (
+                spec[b * ROWS : (b + 1) * ROWS]
+            )
 
 
 def screen(spec_ref, low_ref, wide_ref, column_ref, rows):
@@ -155,61 +160,71 @@
         spec_ref[:rows, lanes] = result.astype(jnp.bfloat16)
 
 
-def inverse(spec_ref, plane_ref, scratch, rows, use):
+def inverse(spec_ref, first_row, plane_ref, scratch, use):
     for first in range(0, BLOCKS, CHUNK):
         operand = jnp.concatenate(
-            [spec_ref[:rows, lane_block(first + b)] for b in range(CHUNK)], axis=0
+            [
+                spec_ref[first_row : first_row + ROWS, lane_block(first + b)]
+                for b in range(CHUNK)
+            ],
+            axis=0,
         )
         both = jnp.dot(operand, plane_ref[:LANES], preferred_element_type=jnp.float32)
-        scratch[first * rows : (first + CHUNK) * rows, :] = both[:, :LANES] + both[:, LANES:]
-    for tile in range(rows // 8):
-        fields = [scratch[b * rows + 8 * tile : b * rows + 8 * tile + 8, :] for b in range(BLOCKS)]
-        slab, row = divmod(8 * tile, ROWS)
+        scratch[first * ROWS : (first + CHUNK) * ROWS, :] = both[:, :LANES] + both[:, LANES:]
+    for tile in range(ROWS // 8):
+        fields = [
+            scratch[b * ROWS + 8 * tile : b * ROWS + 8 * tile + 8, :] for b in range(BLOCKS)
+        ]
         for b, item in enumerate(hartley(twist(fields))):
-            use(slab, slice(row, row + 8), lane_block(b), item)
-
-
-def copy_kernel(code_ref, out_ref):
-    out_ref[...] = code_ref[...]
-
-
-def pair_kernel(cross_ref, same_ref, beside_code, psi_ref, plane_ref, low_ref, wide_ref,
-                column_ref, part_out, field_out, beside_out, same_out, cross_out,
-                other, spec, scratch, sums):
-    other[0] = decoded(same_ref[...])
-    other[1] = decoded(cross_ref[...])
+            use(slice(8 * tile, 8 * tile + 8), lane_block(b), item)
+
+
+def near_kernel(same_ref, psi_ref, plane_ref, same_out, spec_out, scratch):
+    same_out[...] = decoded(same_ref[...])
+    forward(psi_ref.at[0], same_out, plane_ref, spec_out, 0, scratch)
+
+
+def pair_kernel(cross_ref, beside_code, spec_in, plane_ref, low_ref, wide_ref, column_ref,
+                field_out, spec_out, beside_out, cross_out, other, spec, scratch, sums):
+    spec[:ROWS] = spec_in[...]
+    other[...] = decoded(cross_ref[:, :PLANE])
     field_out[...] = decoded(beside_code[:, :PLANE])
-    band = (psi_ref.at[0], field_out)
-    forward(band, (other.at[0], other.at[1]), plane_ref, spec, scratch)
+    forward(field_out, other, plane_ref, spec, ROWS, scratch)
     screen(spec, low_ref, wide_ref, column_ref, NG)
-
-    def use(slab, rows, lanes, item):
-        part = other[slab, rows, lanes] * item
-        if slab == 0:
-            part_out[rows, lanes] = part
-        else:
-            sums[2, rows, lanes] = part
-        sums[slab, rows, lanes] = band[slab][rows, lanes] * item
-
-    inverse(spec, plane_ref, scratch, NG, use)
-    same_out[...] = sums[0].astype(jnp.bfloat16)
-    cross_out[...] = sums[1].astype(jnp.bfloat16)
-    beside_out[...] = sums[2].astype(jnp.bfloat16)
+    spec_out[...] = spec[:ROWS]
+
+    def use(rows, lanes, item):
+        sums[0, rows, lanes] = other[rows, lanes] * item
+        sums[1, rows, lanes] = field_out[rows, lanes] * item
+
+    inverse(spec, ROWS, plane_ref, scratch, use)
+    beside_out[...] = sums[0].astype(jnp.bfloat16)
+    cross_out[:, :PLANE] = sums[1].astype(jnp.bfloat16)
+    cross_out[:, PLANE:] = jnp.zeros((ROWS, LANES), jnp.bfloat16)
+
+
+def same_kernel(spec_ref, plane_ref, psi_ref, other_ref, part_out, same_out, scratch, total):
+    def use(rows, lanes, item):
+        part_out[rows, lanes] = other_ref[rows, lanes] * item
+        total[rows, lanes] = psi_ref[0, rows, lanes] * item
+
+    inverse(spec_ref, 0, plane_ref, scratch, use)
+    same_out[...] = total[...].astype(jnp.bfloat16)
 
 
 def self_kernel(psi_ref, mine_ref, beside_code, field_ref, plane_ref, low_ref, wide_ref,
                 column_ref, part_ref, total_out, spec, scratch):
-    band = (psi_ref.at[0], field_ref)
-    forward(band, band, plane_ref, spec, scratch)
+    forward(psi_ref.at[0], psi_ref.at[0], plane_ref, spec, 0, scratch)
+    forward(field_ref, field_ref, plane_ref, spec, ROWS, scratch)
     first = lax.broadcasted_iota(jnp.int32, (ROWS, LANES), 1) == 0
     for rows, ref in ((slice(0, ROWS), mine_ref), (slice(ROWS, NG), beside_code)):
         spec[rows, :LANES] = jnp.where(first, ref[:, PLANE:], spec[rows, :LANES])
     screen(spec, low_ref, wide_ref, column_ref, ROWS)
 
-    def use(slab, rows, lanes, item):
+    def use(rows, lanes, item):
         total_out[rows, lanes] = part_ref[rows, lanes] + psi_ref[0, rows, lanes] * item
 
-    inverse(spec, plane_ref, scratch, ROWS, use)
+    inverse(spec, 0, plane_ref, scratch, use)
 
 
 vmem = pl.BlockSpec(memory_space=pltpu.VMEM)
@@ -253,30 +268,39 @@
     sent = shape((ROWS, PLANE), jnp.bfloat16)
     field = shape((ROWS, PLANE), jnp.float32)
     spec = pltpu.VMEM((NG, PLANE), jnp.bfloat16)
-    work = pltpu.VMEM((BLOCKS * NG, LANES), jnp.float32)
+    work = pltpu.VMEM((BLOCKS * ROWS, LANES), jnp.float32)
     marks = shape((ROWS, PLANE + LANES), jnp.bfloat16)
 
-    code, marked = call(encode_kernel, (sent, marks), orbitals)
+    code, wide = call(
+        encode_kernel, (sent, shape((ROWS, PLANE + 2 * LANES), jnp.bfloat16)), orbitals
+    )
+    marked = call(
+        mark_kernel, marks, orbitals, code,
+        scratch=[pltpu.VMEM((BLOCKS * ROWS, LANES), jnp.float32)],
+    )
     same = lax.ppermute(code, axes, route(False))
-    cross = lax.ppermute(code, axes, route(True))
-    marked = call(copy_kernel, marks, marked)
+    cross = lax.ppermute(wide, axes, route(True))
     beside = lax.ppermute(marked, "grid", swap)
-    part, partner, beside_share, same, cross = call(
-        pair_kernel, (field, field, sent, sent, sent),
-        cross, same, beside, orbitals, *tables,
+    other, top = call(near_kernel, (field, sent), same, orbitals, stacked, scratch=[work])
+    partner, top, beside_share, cross = call(
+        pair_kernel, (field, sent, sent, marks), cross, beside, top, *tables,
         scratch=[
-            pltpu.VMEM((2, ROWS, PLANE), jnp.float32), spec, work,
-            pltpu.VMEM((3, ROWS, PLANE), jnp.float32),
+            pltpu.VMEM((ROWS, PLANE), jnp.float32), spec, work,
+            pltpu.VMEM((2, ROWS, PLANE), jnp.float32),
         ],
+    )
+    part, same = call(
+        same_kernel, (field, sent), top, stacked, orbitals, other,
+        scratch=[work, pltpu.VMEM((ROWS, PLANE), jnp.float32)],
     )
     total = call(
         self_kernel, field, orbitals, marked, beside, partner, *tables, part,
         scratch=[spec, work],
     )
     for share in (
-        lax.ppermute(cross, axes, home(True)),
+        lax.ppermute(cross, axes, home(True))[:, :PLANE],
+        lax.ppermute(beside_share, "grid", swap),
         lax.ppermute(same, axes, home(False)),
-        lax.ppermute(beside_share, "grid", swap),
     ):
         total = total + share.astype(jnp.float32)
     return -total[None]

time: 51.3 us -> 48.9 us (0.953)
  waiting for transfers between devices: 17.3 us -> 7.43 us
  starting transfers between devices: 26.9 us -> 33.7 us
  Pallas kernels: 4.74 us -> 5.33 us
    ppermute x2, waiting for transfers between devices: 11.9 us -> 0.01 us  [the longest x1 0.01 us: on_device(): cross = lax.ppermute(wide, axes, route(True))]
    ppermute x2, starting transfers between devices: 13.5 us -> 21.9 us  [the longest x1 16.1 us: on_device(): lax.ppermute(cross, axes, home(True))[:, :PLANE]]
    ppermute x1, waiting for transfers between devices: 0.16 us -> 3.29 us  [on_device(): same = lax.ppermute(code, axes, route(False))]
    ppermute x1, starting transfers between devices: 4.08 us -> 2.86 us  [on_device(): beside = lax.ppermute(marked, 'grid', swap)]
    ppermute x1, starting transfers between devices: 1.92 us -> 2.8 us  [on_device(): lax.ppermute(same, axes, home(False))]
    ppermute x1, starting transfers between devices: 4.84 us -> 4.04 us  [on_device(): same = lax.ppermute(code, axes, route(False))]
    ppermute x1, waiting for transfers between devices: 4.03 us -> 3.25 us  [on_device(): lax.ppermute(beside_share, 'grid', swap)]
    pallas_call x4 -> x6, Pallas kernels: 4.74 us -> 5.33 us  [call(): pl.pallas_call(kernel, out_shape=outs, in_specs=[vmem] * len(args), out_s...]
  transfers between devices with their start and end apart: 6 -> 6, of which waited for: 5 -> 3; matrix products, arithmetic and copies ran while one was open for 0% -> 0% of each run, Pallas kernels for 4% -> 7%
where the time goes in v2:
time: 48.9 us; the launch traced here: 48.6 us
  starting transfers between devices  33.7 us (69%)
  waiting for transfers between devices  7.43 us (15%)
  Pallas kernels  5.33 us (11%)
  local copies, waits for them, and re-layouts  1.09 us (2%)
  other arithmetic  0.93 us (2%)
    ppermute x1, starting transfers between devices, on_device(): lax.ppermute(cross, axes, home(True))[:, :PLANE]  16.1 us
    ppermute x1, starting transfers between devices, on_device(): cross = lax.ppermute(wide, axes, route(True))  5.76 us
    pallas_call x6, Pallas kernels, call(): pl.pallas_call(kernel, out_shape=outs, in_specs=[vmem] * len(args), out_s...  5.33 us
    ppermute x1, starting transfers between devices, on_device(): same = lax.ppermute(code, axes, route(False))  4.04 us
    ppermute x1, waiting for transfers between devices, on_device(): same = lax.ppermute(code, axes, route(False))  3.29 us
    ppermute x1, waiting for transfers between devices, on_device(): lax.ppermute(beside_share, 'grid', swap)  3.25 us
    ppermute x1, starting transfers between devices, on_device(): beside = lax.ppermute(marked, 'grid', swap)  2.86 us
    ppermute x1, starting transfers between devices, on_device(): lax.ppermute(same, axes, home(False))  2.8 us
  transfers between devices with their start and end apart: 6, of which 3 were waited for; matrix products, arithmetic and copies ran while one was open for 0% of the time, Pallas kernels for 7%

profile of v2, /device:TPU:1, one launch (start us, length us, event | category | flops | bytes accessed | tf_op | source)
XLA Modules:
  0.0 48.6 jit_solution(6664579401686393672)
XLA Ops:
  0.0 0.0 copy-start
  0.0 1.0 %copy-done = f32[1,32,4096]{2,1,0:T(8,128)S(1)} copy-done((f32[1,32,4096]{2,1,0:T(8,128)S(1)}, f32[1,32,4096]{2,1,0:T(8,128)}, u32[]{:S(2)}) %copy-start) | copy-done | bytes 524312
  1.0 0.1 shard_map.55
  1.1 5.8 %collective-permute-start.1 = (bf16[32,4352]{1,0:T(8,128)(2,1)S(1)}, bf16[32,4352]{1,0:T(8,128)(2,1)S(1)}, u32[]{:S(2)}, u32[]{:S(2)}) collective-permute-start(bf16[32,4352]{1,0:T(8,128)(2,1)S(1)} %get-tuple-element.16), channel_id=1, source_target_pairs={{511,0},{508,1},{1,2},{510,3},{3,4},{0,5},{5,6},{2,7},{7,8},{4,9},... | collective-permute-start | bytes 835592 | tf_op jit(solution)/shard_map/ppermute | solution.py:282
  6.9 0.0 copy-start.2
  6.9 0.6 %shard_map.56.mine_ref = bf16[32,4224]{1,0:T(8,128)(2,1)S(1)} custom-call(f32[1,32,4096]{2,1,0:T(8,128)S(1)} %copy-done, bf16[32,4096]{1,0:T(8,128)(2,1)S(1)} %get-tuple-element.15.code_ref), custom_call_target="tpu_custom_call" | custom-call | tf_op jit(solution)/shard_map/pallas_call | solution.py:239
  7.5 0.0 copy-start.3
  7.5 0.0 copy-start.4
  7.5 0.0 copy-start.5
  7.5 2.9 %collective-permute-start = (bf16[32,4224]{1,0:T(8,128)(2,1)S(1)}, bf16[32,4224]{1,0:T(8,128)(2,1)S(1)}, u32[]{:S(2)}, u32[]{:S(2)}) collective-permute-start(bf16[32,4224]{1,0:T(8,128)(2,1)S(1)} %shard_map.56.mine_ref), channel_id=1, source_target_pairs={{0,1},{1,0},{2,3},{3,2},{4,5},{5,4},{6,7},{7,6},{8,9},{9,8},{10,11... | collective-permute-start | bytes 811016 | tf_op jit(solution)/shard_map/ppermute | solution.py:283
  10.4 4.0 %collective-permute-start.2 = (bf16[32,4096]{1,0:T(8,128)(2,1)S(1)}, bf16[32,4096]{1,0:T(8,128)(2,1)S(1)}, u32[]{:S(2)}, u32[]{:S(2)}) collective-permute-start(bf16[32,4096]{1,0:T(8,128)(2,1)S(1)} %get-tuple-element.15.code_ref), channel_id=1, source_target_pairs={{510,0},{509,1},{0,2},{511,3},{2,4},{1,5},{4,6},{3,7},{6,8},{5,9},... | collective-permute-start | bytes 786440 | tf_op jit(solution)/shard_map/ppermute | solution.py:281
  14.4 3.3 %collective-permute-done.2.same_ref = bf16[32,4096]{1,0:T(8,128)(2,1)S(1)} collective-permute-done((bf16[32,4096]{1,0:T(8,128)(2,1)S(1)}, bf16[32,4096]{1,0:T(8,128)(2,1)S(1)}, u32[]{:S(2)}, u32[]{:S(2)}) %collective-permute-start.2) | collective-permute-done | bytes 262176 | tf_op jit(solution)/shard_map/ppermute | solution.py:281
  17.7 0.0 copy-done.2
  17.7 0.5 %shard_map.57 = (f32[32,4096]{1,0:T(8,128)S(1)}, bf16[32,4096]{1,0:T(8,128)(2,1)S(1)}) custom-call(bf16[32,4096]{1,0:T(8,128)(2,1)S(1)} %collective-permute-done.2.same_ref, f32[1,32,4096]{2,1,0:T(8,128)S(1)} %copy-done, bf16[256,256]{1,0:T(8,128)(2,1)S(1)} %copy-done.2), custom_call_target="tpu_custom_call" | custom-call | tf_op jit(solution)/shard_map/pallas_call | solution.py:239
  18.2 0.0 copy-start.1
  18.2 0.0 collective-permute-done.beside_code
  18.3 0.0 collective-permute-done.1.cross_ref
  18.3 0.0 copy-done.3
  18.3 0.0 copy-done.4
  18.3 0.0 copy-done.5
  18.3 1.8 %shard_map.58 = (f32[32,4096]{1,0:T(8,128)S(1)}, bf16[32,4096]{1,0:T(8,128)(2,1)S(1)}, bf16[32,4096]{1,0:T(8,128)(2,1)S(1)}, bf16[32,4224]{1,0:T(8,128)(2,1)S(1)}) custom-call(bf16[32,4352]{1,0:T(8,128)(2,1)S(1)} %collective-permute-done.1.cross_ref, bf16[32,4224]{1,0:T(8,128)(2,1)S(1)} %collective-permute-done.beside_code, ...), custom_call_target="tpu_custom_call" | custom-call | tf_op jit(solution)/shard_map/pallas_call | solution.py:239
  20.1 16.1 %collective-permute-start.3 = (bf16[32,4224]{1,0:T(8,128)(2,1)S(1)}, bf16[32,4224]{1,0:T(8,128)(2,1)S(1)}, u32[]{:S(2)}, u32[]{:S(2)}) collective-permute-start(bf16[32,4224]{1,0:T(8,128)(2,1)S(1)} %get-tuple-element.22), channel_id=1, source_target_pairs={{0,511},{1,508},{2,1},{3,510},{4,3},{5,0},{6,5},{7,2},{8,7},{9,4},... | collective-permute-start | bytes 811016 | tf_op jit(solution)/shard_map/ppermute | solution.py:301
  36.2 0.0 copy-done.1
  36.2 0.5 %shard_map.59 = (f32[32,4096]{1,0:T(8,128)S(1)}, bf16[32,4096]{1,0:T(8,128)(2,1)S(1)}) custom-call(bf16[32,4096]{1,0:T(8,128)(2,1)S(1)} %get-tuple-element.19.spec_ref, bf16[256,256]{1,0:T(8,128)(2,1)S(1)} %copy-done.2, f32[1,32,4096]{2,1,0:T(8,128)S(1)} %copy-done.1, f32[32,4096]{1,0:T(8,128)S(1)} %get-tuple-element.20.other_ref), custom_call_target="tpu_custom_call" | custom-call | tf_op jit(solution)/shard_map/pallas_call | solution.py:239
  36.7 2.8 %collective-permute-start.5 = (bf16[32,4096]{1,0:T(8,128)(2,1)S(1)}, bf16[32,4096]{1,0:T(8,128)(2,1)S(1)}, u32[]{:S(2)}, u32[]{:S(2)}) collective-permute-start(bf16[32,4096]{1,0:T(8,128)(2,1)S(1)} %get-tuple-element.24), channel_id=1, source_target_pairs={{0,510},{1,509},{2,0},{3,511},{4,2},{5,1},{6,4},{7,3},{8,6},{9,5},... | collective-permute-start | bytes 786440 | tf_op jit(solution)/shard_map/ppermute | solution.py:303
  39.5 2.1 %collective-permute-start.4 = (bf16[32,4096]{1,0:T(8,128)(2,1)S(1)}, bf16[32,4096]{1,0:T(8,128)(2,1)S(1)}, u32[]{:S(2)}, u32[]{:S(2)}) collective-permute-start(bf16[32,4096]{1,0:T(8,128)(2,1)S(1)} %get-tuple-element.23), channel_id=1, source_target_pairs={{0,1},{1,0},{2,3},{3,2},{4,5},{5,4},{6,7},{7,6},{8,9},{9,8},{10,11... | collective-permute-start | bytes 786440 | tf_op jit(solution)/shard_map/ppermute | solution.py:302
  41.6 1.9 %shard_map.60 = f32[32,4096]{1,0:T(8,128)S(1)} custom-call(f32[1,32,4096]{2,1,0:T(8,128)S(1)} %copy-done.1, bf16[32,4224]{1,0:T(8,128)(2,1)S(1)} %shard_map.56.mine_ref, bf16[32,4224]{1,0:T(8,128)(2,1)S(1)} %collective-permute-done.beside_code, f32[32,4096]{1,0:T(8,128)S(1)} %get-tuple-element.18.field_ref, bf16[256,256]{1,0:T(8,128)(2,1)S(1)} %copy-done.2, ...), custom_call_target="tpu_custom_call" | custom-call | tf_op jit(solution)/shard_map/pallas_call | solution.py:239
  43.5 0.9 %collective-permute-done.5 = bf16[32,4096]{1,0:T(8,128)(2,1)S(1)} collective-permute-done((bf16[32,4096]{1,0:T(8,128)(2,1)S(1)}, bf16[32,4096]{1,0:T(8,128)(2,1)S(1)}, u32[]{:S(2)}, u32[]{:S(2)}) %collective-permute-start.5) | collective-permute-done | bytes 262176 | tf_op jit(solution)/shard_map/ppermute | solution.py:303
  44.4 3.3 %collective-permute-done.4 = bf16[32,4096]{1,0:T(8,128)(2,1)S(1)} collective-permute-done((bf16[32,4096]{1,0:T(8,128)(2,1)S(1)}, bf16[32,4096]{1,0:T(8,128)(2,1)S(1)}, u32[]{:S(2)}, u32[]{:S(2)}) %collective-permute-start.4) | collective-permute-done | bytes 262176 | tf_op jit(solution)/shard_map/ppermute | solution.py:302
  47.7 0.0 collective-permute-done.3
  47.7 0.9 %negate_bitcast_fusion = f32[1,32,4096]{2,1,0:T(8,128)} fusion(bf16[32,4096]{1,0:T(8,128)(2,1)S(1)} %collective-permute-done.5, bf16[32,4096]{1,0:T(8,128)(2,1)S(1)} %collective-permute-done.4, f32[32,4096]{1,0:T(8,128)S(1)} %shard_map.60, bf16[32,4224]{1,0:T(8,128)(2,1)S(1)} %collective-permute-done.3), kind=kLoop, calls=%fused_computation | loop fusion | flops 917504 | bytes 1835008 | tf_op jit(solution)/shard_map/neg | solution.py:306
Async XLA Ops:
  0.0 1.0 %copy-start = (f32[1,32,4096]{2,1,0:T(8,128)S(1)}, f32[1,32,4096]{2,1,0:T(8,128)}, u32[]{:S(2)}) copy-start(f32[1,32,4096]{2,1,0:T(8,128)} %psi_ref.9) | copy-start | bytes 1572868
  1.1 17.1 %collective-permute-start.1 = (bf16[32,4352]{1,0:T(8,128)(2,1)S(1)}, bf16[32,4352]{1,0:T(8,128)(2,1)S(1)}, u32[]{:S(2)}, u32[]{:S(2)}) collective-permute-start(bf16[32,4352]{1,0:T(8,128)(2,1)S(1)} %get-tuple-element.16), channel_id=1, source_target_pairs={{511,0},{508,1},{1,2},{510,3},{3,4},{0,5},{5,6},{2,7},{7,8},{4,9},... | collective-permute-start | bytes 835592 | tf_op jit(solution)/shard_map/ppermute | solution.py:282
  6.9 10.8 %copy-start.2 = (bf16[256,256]{1,0:T(8,128)(2,1)S(1)}, bf16[256,256]{1,0:T(8,128)(2,1)}, u32[]{:S(2)}) copy-start(bf16[256,256]{1,0:T(8,128)(2,1)} %constant.13.plane_ref) | copy-start | bytes 393220
  7.5 10.8 %copy-start.3 = (bf16[64,192]{1,0:T(8,128)(2,1)S(1)}, bf16[64,192]{1,0:T(8,128)(2,1)}, u32[]{:S(2)}) copy-start(bf16[64,192]{1,0:T(8,128)(2,1)} %constant.10.clone.wide_ref) | copy-start | bytes 73732
  7.5 10.8 %copy-start.4 = (f32[1,4096]{1,0:T(1,128)S(1)}, f32[1,4096]{1,0:T(1,128)}, u32[]{:S(2)}) copy-start(f32[1,4096]{1,0:T(1,128)} %constant.11.clone.column_ref) | copy-start | bytes 49156
  7.5 10.8 %copy-start.5 = (bf16[64,64]{1,0:T(8,128)(2,1)S(1)}, bf16[64,64]{1,0:T(8,128)(2,1)}, u32[]{:S(2)}) copy-start(bf16[64,64]{1,0:T(8,128)(2,1)} %constant.9.clone.low_ref) | copy-start | bytes 24580
  7.5 10.7 %collective-permute-start = (bf16[32,4224]{1,0:T(8,128)(2,1)S(1)}, bf16[32,4224]{1,0:T(8,128)(2,1)S(1)}, u32[]{:S(2)}, u32[]{:S(2)}) collective-permute-start(bf16[32,4224]{1,0:T(8,128)(2,1)S(1)} %shard_map.56.mine_ref), channel_id=1, source_target_pairs={{0,1},{1,0},{2,3},{3,2},{4,5},{5,4},{6,7},{7,6},{8,9},{9,8},{10,11... | collective-permute-start | bytes 811016 | tf_op jit(solution)/shard_map/ppermute | solution.py:283
  10.4 7.3 %collective-permute-start.2 = (bf16[32,4096]{1,0:T(8,128)(2,1)S(1)}, bf16[32,4096]{1,0:T(8,128)(2,1)S(1)}, u32[]{:S(2)}, u32[]{:S(2)}) collective-permute-start(bf16[32,4096]{1,0:T(8,128)(2,1)S(1)} %get-tuple-element.15.code_ref), channel_id=1, source_target_pairs={{510,0},{509,1},{0,2},{511,3},{2,4},{1,5},{4,6},{3,7},{6,8},{5,9},... | collective-permute-start | bytes 786440 | tf_op jit(solution)/shard_map/ppermute | solution.py:281
  18.2 18.0 %copy-start.1 = (f32[1,32,4096]{2,1,0:T(8,128)S(1)}, f32[1,32,4096]{2,1,0:T(8,128)}, u32[]{:S(2)}) copy-start(f32[1,32,4096]{2,1,0:T(8,128)} %psi_ref.9) | copy-start | bytes 1572868
  20.1 27.6 %collective-permute-start.3 = (bf16[32,4224]{1,0:T(8,128)(2,1)S(1)}, bf16[32,4224]{1,0:T(8,128)(2,1)S(1)}, u32[]{:S(2)}, u32[]{:S(2)}) collective-permute-start(bf16[32,4224]{1,0:T(8,128)(2,1)S(1)} %get-tuple-element.22), channel_id=1, source_target_pairs={{0,511},{1,508},{2,1},{3,510},{4,3},{5,0},{6,5},{7,2},{8,7},{9,4},... | collective-permute-start | bytes 811016 | tf_op jit(solution)/shard_map/ppermute | solution.py:301
  36.7 7.7 %collective-permute-start.5 = (bf16[32,4096]{1,0:T(8,128)(2,1)S(1)}, bf16[32,4096]{1,0:T(8,128)(2,1)S(1)}, u32[]{:S(2)}, u32[]{:S(2)}) collective-permute-start(bf16[32,4096]{1,0:T(8,128)(2,1)S(1)} %get-tuple-element.24), channel_id=1, source_target_pairs={{0,510},{1,509},{2,0},{3,511},{4,2},{5,1},{6,4},{7,3},{8,6},{9,5},... | collective-permute-start | bytes 786440 | tf_op jit(solution)/shard_map/ppermute | solution.py:303
  39.5 8.1 %collective-permute-start.4 = (bf16[32,4096]{1,0:T(8,128)(2,1)S(1)}, bf16[32,4096]{1,0:T(8,128)(2,1)S(1)}, u32[]{:S(2)}, u32[]{:S(2)}) collective-permute-start(bf16[32,4096]{1,0:T(8,128)(2,1)S(1)} %get-tuple-element.23), channel_id=1, source_target_pairs={{0,1},{1,0},{2,3},{3,2},{4,5},{5,4},{6,7},{7,6},{8,9},{9,8},{10,11... | collective-permute-start | bytes 786440 | tf_op jit(solution)/shard_map/ppermute | solution.py:302

commit v3 on v2

--- a/solution.py
+++ b/solution.py
@@ -16,8 +16,8 @@
 LANES = 2 * NG
 BLOCKS = PLANE // LANES
 CODE = 64.0
-CHUNK = 8
-WIDTH = 1024
+CHUNK = 16
+WIDTH = 2048
 coulomb = 46.9 * 46.9 / math.pi
 
 

time: 48.9 us -> 48.8 us (level)
  no operation moved by 1% of the time
where the time goes in v3:
time: 48.8 us; the launch traced here: 48.4 us
  starting transfers between devices  33.6 us (69%)
  waiting for transfers between devices  7.64 us (16%)
  Pallas kernels  4.96 us (10%)
  local copies, waits for them, and re-layouts  1.09 us (2%)
  other arithmetic  0.93 us (2%)
    ppermute x1, starting transfers between devices, on_device(): lax.ppermute(cross, axes, home(True))[:, :PLANE]  16.2 us
    ppermute x1, starting transfers between devices, on_device(): cross = lax.ppermute(wide, axes, route(True))  5.76 us
    pallas_call x6, Pallas kernels, call(): pl.pallas_call(kernel, out_shape=outs, in_specs=[vmem] * len(args), out_s...  4.96 us
    ppermute x1, starting transfers between devices, on_device(): same = lax.ppermute(code, axes, route(False))  4.04 us
    ppermute x1, waiting for transfers between devices, on_device(): same = lax.ppermute(code, axes, route(False))  3.29 us
    ppermute x1, waiting for transfers between devices, on_device(): lax.ppermute(beside_share, 'grid', swap)  3.15 us
    ppermute x1, starting transfers between devices, on_device(): beside = lax.ppermute(marked, 'grid', swap)  2.86 us
    ppermute x1, starting transfers between devices, on_device(): lax.ppermute(same, axes, home(False))  2.69 us
  transfers between devices with their start and end apart: 6, of which 3 were waited for; matrix products, arithmetic and copies ran while one was open for 0% of the time, Pallas kernels for 7%

profile of v3, /device:TPU:1, one launch (start us, length us, event | category | flops | bytes accessed | tf_op | source)
XLA Modules:
  0.0 48.4 jit_solution(8375311436233195883)
XLA Ops:
  0.0 0.0 copy-start
  0.0 1.0 %copy-done = f32[1,32,4096]{2,1,0:T(8,128)S(1)} copy-done((f32[1,32,4096]{2,1,0:T(8,128)S(1)}, f32[1,32,4096]{2,1,0:T(8,128)}, u32[]{:S(2)}) %copy-start) | copy-done | bytes 524312
  1.0 0.1 shard_map.55
  1.1 5.8 %collective-permute-start.1 = (bf16[32,4352]{1,0:T(8,128)(2,1)S(1)}, bf16[32,4352]{1,0:T(8,128)(2,1)S(1)}, u32[]{:S(2)}, u32[]{:S(2)}) collective-permute-start(bf16[32,4352]{1,0:T(8,128)(2,1)S(1)} %get-tuple-element.16), channel_id=1, source_target_pairs={{511,0},{508,1},{1,2},{510,3},{3,4},{0,5},{5,6},{2,7},{7,8},{4,9},... | collective-permute-start | bytes 835592 | tf_op jit(solution)/shard_map/ppermute | solution.py:282
  6.9 0.0 copy-start.2
  6.9 0.6 %shard_map.56.mine_ref = bf16[32,4224]{1,0:T(8,128)(2,1)S(1)} custom-call(f32[1,32,4096]{2,1,0:T(8,128)S(1)} %copy-done, bf16[32,4096]{1,0:T(8,128)(2,1)S(1)} %get-tuple-element.15.code_ref), custom_call_target="tpu_custom_call" | custom-call | tf_op jit(solution)/shard_map/pallas_call | solution.py:239
  7.5 0.0 copy-start.3
  7.5 0.0 copy-start.4
  7.5 0.0 copy-start.5
  7.5 2.9 %collective-permute-start = (bf16[32,4224]{1,0:T(8,128)(2,1)S(1)}, bf16[32,4224]{1,0:T(8,128)(2,1)S(1)}, u32[]{:S(2)}, u32[]{:S(2)}) collective-permute-start(bf16[32,4224]{1,0:T(8,128)(2,1)S(1)} %shard_map.56.mine_ref), channel_id=1, source_target_pairs={{0,1},{1,0},{2,3},{3,2},{4,5},{5,4},{6,7},{7,6},{8,9},{9,8},{10,11... | collective-permute-start | bytes 811016 | tf_op jit(solution)/shard_map/ppermute | solution.py:283
  10.4 4.0 %collective-permute-start.2 = (bf16[32,4096]{1,0:T(8,128)(2,1)S(1)}, bf16[32,4096]{1,0:T(8,128)(2,1)S(1)}, u32[]{:S(2)}, u32[]{:S(2)}) collective-permute-start(bf16[32,4096]{1,0:T(8,128)(2,1)S(1)} %get-tuple-element.15.code_ref), channel_id=1, source_target_pairs={{510,0},{509,1},{0,2},{511,3},{2,4},{1,5},{4,6},{3,7},{6,8},{5,9},... | collective-permute-start | bytes 786440 | tf_op jit(solution)/shard_map/ppermute | solution.py:281
  14.4 3.3 %collective-permute-done.2.same_ref = bf16[32,4096]{1,0:T(8,128)(2,1)S(1)} collective-permute-done((bf16[32,4096]{1,0:T(8,128)(2,1)S(1)}, bf16[32,4096]{1,0:T(8,128)(2,1)S(1)}, u32[]{:S(2)}, u32[]{:S(2)}) %collective-permute-start.2) | collective-permute-done | bytes 262176 | tf_op jit(solution)/shard_map/ppermute | solution.py:281
  17.7 0.0 copy-done.2
  17.7 0.5 %shard_map.57 = (f32[32,4096]{1,0:T(8,128)S(1)}, bf16[32,4096]{1,0:T(8,128)(2,1)S(1)}) custom-call(bf16[32,4096]{1,0:T(8,128)(2,1)S(1)} %collective-permute-done.2.same_ref, f32[1,32,4096]{2,1,0:T(8,128)S(1)} %copy-done, bf16[256,256]{1,0:T(8,128)(2,1)S(1)} %copy-done.2), custom_call_target="tpu_custom_call" | custom-call | tf_op jit(solution)/shard_map/pallas_call | solution.py:239
  18.3 0.0 copy-start.1
  18.3 0.0 collective-permute-done.beside_code
  18.3 0.0 collective-permute-done.1.cross_ref
  18.3 0.0 copy-done.3
  18.3 0.0 copy-done.4
  18.3 0.0 copy-done.5
  18.3 1.6 %shard_map.58 = (f32[32,4096]{1,0:T(8,128)S(1)}, bf16[32,4096]{1,0:T(8,128)(2,1)S(1)}, bf16[32,4096]{1,0:T(8,128)(2,1)S(1)}, bf16[32,4224]{1,0:T(8,128)(2,1)S(1)}) custom-call(bf16[32,4352]{1,0:T(8,128)(2,1)S(1)} %collective-permute-done.1.cross_ref, bf16[32,4224]{1,0:T(8,128)(2,1)S(1)} %collective-permute-done.beside_code, ...), custom_call_target="tpu_custom_call" | custom-call | tf_op jit(solution)/shard_map/pallas_call | solution.py:239
  19.9 16.2 %collective-permute-start.3 = (bf16[32,4224]{1,0:T(8,128)(2,1)S(1)}, bf16[32,4224]{1,0:T(8,128)(2,1)S(1)}, u32[]{:S(2)}, u32[]{:S(2)}) collective-permute-start(bf16[32,4224]{1,0:T(8,128)(2,1)S(1)} %get-tuple-element.22), channel_id=1, source_target_pairs={{0,511},{1,508},{2,1},{3,510},{4,3},{5,0},{6,5},{7,2},{8,7},{9,4},... | collective-permute-start | bytes 811016 | tf_op jit(solution)/shard_map/ppermute | solution.py:301
  36.1 0.0 copy-done.1
  36.1 0.5 %shard_map.59 = (f32[32,4096]{1,0:T(8,128)S(1)}, bf16[32,4096]{1,0:T(8,128)(2,1)S(1)}) custom-call(bf16[32,4096]{1,0:T(8,128)(2,1)S(1)} %get-tuple-element.19.spec_ref, bf16[256,256]{1,0:T(8,128)(2,1)S(1)} %copy-done.2, f32[1,32,4096]{2,1,0:T(8,128)S(1)} %copy-done.1, f32[32,4096]{1,0:T(8,128)S(1)} %get-tuple-element.20.other_ref), custom_call_target="tpu_custom_call" | custom-call | tf_op jit(solution)/shard_map/pallas_call | solution.py:239
  36.7 2.7 %collective-permute-start.5 = (bf16[32,4096]{1,0:T(8,128)(2,1)S(1)}, bf16[32,4096]{1,0:T(8,128)(2,1)S(1)}, u32[]{:S(2)}, u32[]{:S(2)}) collective-permute-start(bf16[32,4096]{1,0:T(8,128)(2,1)S(1)} %get-tuple-element.24), channel_id=1, source_target_pairs={{0,510},{1,509},{2,0},{3,511},{4,2},{5,1},{6,4},{7,3},{8,6},{9,5},... | collective-permute-start | bytes 786440 | tf_op jit(solution)/shard_map/ppermute | solution.py:303
  39.4 2.1 %collective-permute-start.4 = (bf16[32,4096]{1,0:T(8,128)(2,1)S(1)}, bf16[32,4096]{1,0:T(8,128)(2,1)S(1)}, u32[]{:S(2)}, u32[]{:S(2)}) collective-permute-start(bf16[32,4096]{1,0:T(8,128)(2,1)S(1)} %get-tuple-element.23), channel_id=1, source_target_pairs={{0,1},{1,0},{2,3},{3,2},{4,5},{5,4},{6,7},{7,6},{8,9},{9,8},{10,11... | collective-permute-start | bytes 786440 | tf_op jit(solution)/shard_map/ppermute | solution.py:302
  41.5 1.7 %shard_map.60 = f32[32,4096]{1,0:T(8,128)S(1)} custom-call(f32[1,32,4096]{2,1,0:T(8,128)S(1)} %copy-done.1, bf16[32,4224]{1,0:T(8,128)(2,1)S(1)} %shard_map.56.mine_ref, bf16[32,4224]{1,0:T(8,128)(2,1)S(1)} %collective-permute-done.beside_code, f32[32,4096]{1,0:T(8,128)S(1)} %get-tuple-element.18.field_ref, bf16[256,256]{1,0:T(8,128)(2,1)S(1)} %copy-done.2, ...), custom_call_target="tpu_custom_call" | custom-call | tf_op jit(solution)/shard_map/pallas_call | solution.py:239
  43.2 1.2 %collective-permute-done.5 = bf16[32,4096]{1,0:T(8,128)(2,1)S(1)} collective-permute-done((bf16[32,4096]{1,0:T(8,128)(2,1)S(1)}, bf16[32,4096]{1,0:T(8,128)(2,1)S(1)}, u32[]{:S(2)}, u32[]{:S(2)}) %collective-permute-start.5) | collective-permute-done | bytes 262176 | tf_op jit(solution)/shard_map/ppermute | solution.py:303
  44.3 3.1 %collective-permute-done.4 = bf16[32,4096]{1,0:T(8,128)(2,1)S(1)} collective-permute-done((bf16[32,4096]{1,0:T(8,128)(2,1)S(1)}, bf16[32,4096]{1,0:T(8,128)(2,1)S(1)}, u32[]{:S(2)}, u32[]{:S(2)}) %collective-permute-start.4) | collective-permute-done | bytes 262176 | tf_op jit(solution)/shard_map/ppermute | solution.py:302
  47.5 0.0 collective-permute-done.3
  47.5 0.9 %negate_bitcast_fusion = f32[1,32,4096]{2,1,0:T(8,128)} fusion(bf16[32,4096]{1,0:T(8,128)(2,1)S(1)} %collective-permute-done.5, bf16[32,4096]{1,0:T(8,128)(2,1)S(1)} %collective-permute-done.4, f32[32,4096]{1,0:T(8,128)S(1)} %shard_map.60, bf16[32,4224]{1,0:T(8,128)(2,1)S(1)} %collective-permute-done.3), kind=kLoop, calls=%fused_computation | loop fusion | flops 917504 | bytes 1835008 | tf_op jit(solution)/shard_map/neg | solution.py:306
Async XLA Ops:
  0.0 1.0 %copy-start = (f32[1,32,4096]{2,1,0:T(8,128)S(1)}, f32[1,32,4096]{2,1,0:T(8,128)}, u32[]{:S(2)}) copy-start(f32[1,32,4096]{2,1,0:T(8,128)} %psi_ref.9) | copy-start | bytes 1572868
  1.1 17.2 %collective-permute-start.1 = (bf16[32,4352]{1,0:T(8,128)(2,1)S(1)}, bf16[32,4352]{1,0:T(8,128)(2,1)S(1)}, u32[]{:S(2)}, u32[]{:S(2)}) collective-permute-start(bf16[32,4352]{1,0:T(8,128)(2,1)S(1)} %get-tuple-element.16), channel_id=1, source_target_pairs={{511,0},{508,1},{1,2},{510,3},{3,4},{0,5},{5,6},{2,7},{7,8},{4,9},... | collective-permute-start | bytes 835592 | tf_op jit(solution)/shard_map/ppermute | solution.py:282
  6.9 10.8 %copy-start.2 = (bf16[256,256]{1,0:T(8,128)(2,1)S(1)}, bf16[256,256]{1,0:T(8,128)(2,1)}, u32[]{:S(2)}) copy-start(bf16[256,256]{1,0:T(8,128)(2,1)} %constant.13.plane_ref) | copy-start | bytes 393220
  7.5 10.8 %copy-start.3 = (bf16[64,192]{1,0:T(8,128)(2,1)S(1)}, bf16[64,192]{1,0:T(8,128)(2,1)}, u32[]{:S(2)}) copy-start(bf16[64,192]{1,0:T(8,128)(2,1)} %constant.10.clone.wide_ref) | copy-start | bytes 73732
  7.5 10.8 %copy-start.4 = (f32[1,4096]{1,0:T(1,128)S(1)}, f32[1,4096]{1,0:T(1,128)}, u32[]{:S(2)}) copy-start(f32[1,4096]{1,0:T(1,128)} %constant.11.clone.column_ref) | copy-start | bytes 49156
  7.5 10.8 %copy-start.5 = (bf16[64,64]{1,0:T(8,128)(2,1)S(1)}, bf16[64,64]{1,0:T(8,128)(2,1)}, u32[]{:S(2)}) copy-start(bf16[64,64]{1,0:T(8,128)(2,1)} %constant.9.clone.low_ref) | copy-start | bytes 24580
  7.5 10.8 %collective-permute-start = (bf16[32,4224]{1,0:T(8,128)(2,1)S(1)}, bf16[32,4224]{1,0:T(8,128)(2,1)S(1)}, u32[]{:S(2)}, u32[]{:S(2)}) collective-permute-start(bf16[32,4224]{1,0:T(8,128)(2,1)S(1)} %shard_map.56.mine_ref), channel_id=1, source_target_pairs={{0,1},{1,0},{2,3},{3,2},{4,5},{5,4},{6,7},{7,6},{8,9},{9,8},{10,11... | collective-permute-start | bytes 811016 | tf_op jit(solution)/shard_map/ppermute | solution.py:283
  10.4 7.3 %collective-permute-start.2 = (bf16[32,4096]{1,0:T(8,128)(2,1)S(1)}, bf16[32,4096]{1,0:T(8,128)(2,1)S(1)}, u32[]{:S(2)}, u32[]{:S(2)}) collective-permute-start(bf16[32,4096]{1,0:T(8,128)(2,1)S(1)} %get-tuple-element.15.code_ref), channel_id=1, source_target_pairs={{510,0},{509,1},{0,2},{511,3},{2,4},{1,5},{4,6},{3,7},{6,8},{5,9},... | collective-permute-start | bytes 786440 | tf_op jit(solution)/shard_map/ppermute | solution.py:281
  18.3 17.9 %copy-start.1 = (f32[1,32,4096]{2,1,0:T(8,128)S(1)}, f32[1,32,4096]{2,1,0:T(8,128)}, u32[]{:S(2)}) copy-start(f32[1,32,4096]{2,1,0:T(8,128)} %psi_ref.9) | copy-start | bytes 1572868
  19.9 27.6 %collective-permute-start.3 = (bf16[32,4224]{1,0:T(8,128)(2,1)S(1)}, bf16[32,4224]{1,0:T(8,128)(2,1)S(1)}, u32[]{:S(2)}, u32[]{:S(2)}) collective-permute-start(bf16[32,4224]{1,0:T(8,128)(2,1)S(1)} %get-tuple-element.22), channel_id=1, source_target_pairs={{0,511},{1,508},{2,1},{3,510},{4,3},{5,0},{6,5},{7,2},{8,7},{9,4},... | collective-permute-start | bytes 811016 | tf_op jit(solution)/shard_map/ppermute | solution.py:301
  36.7 7.7 %collective-permute-start.5 = (bf16[32,4096]{1,0:T(8,128)(2,1)S(1)}, bf16[32,4096]{1,0:T(8,128)(2,1)S(1)}, u32[]{:S(2)}, u32[]{:S(2)}) collective-permute-start(bf16[32,4096]{1,0:T(8,128)(2,1)S(1)} %get-tuple-element.24), channel_id=1, source_target_pairs={{0,510},{1,509},{2,0},{3,511},{4,2},{5,1},{6,4},{7,3},{8,6},{9,5},... | collective-permute-start | bytes 786440 | tf_op jit(solution)/shard_map/ppermute | solution.py:303
  39.4 8.1 %collective-permute-start.4 = (bf16[32,4096]{1,0:T(8,128)(2,1)S(1)}, bf16[32,4096]{1,0:T(8,128)(2,1)S(1)}, u32[]{:S(2)}, u32[]{:S(2)}) collective-permute-start(bf16[32,4096]{1,0:T(8,128)(2,1)S(1)} %get-tuple-element.23), channel_id=1, source_target_pairs={{0,1},{1,0},{2,3},{3,2},{4,5},{5,4},{6,7},{7,6},{8,9},{9,8},{10,11... | collective-permute-start | bytes 786440 | tf_op jit(solution)/shard_map/ppermute | solution.py:302

commit v4 on v3

--- a/solution.py
+++ b/solution.py
@@ -179,15 +179,15 @@
             use(slice(8 * tile, 8 * tile + 8), lane_block(b), item)
 
 
-def near_kernel(same_ref, psi_ref, plane_ref, same_out, spec_out, scratch):
+def near_kernel(same_ref, cross_ref, psi_ref, plane_ref, same_out, cross_out, spec_out, scratch):
     same_out[...] = decoded(same_ref[...])
+    cross_out[...] = decoded(cross_ref[:, :PLANE])
     forward(psi_ref.at[0], same_out, plane_ref, spec_out, 0, scratch)
 
 
-def pair_kernel(cross_ref, beside_code, spec_in, plane_ref, low_ref, wide_ref, column_ref,
-                field_out, spec_out, beside_out, cross_out, other, spec, scratch, sums):
+def pair_kernel(other, beside_code, spec_in, plane_ref, low_ref, wide_ref, column_ref,
+                field_out, spec_out, beside_out, cross_out, spec, scratch, sums):
     spec[:ROWS] = spec_in[...]
-    other[...] = decoded(cross_ref[:, :PLANE])
     field_out[...] = decoded(beside_code[:, :PLANE])
     forward(field_out, other, plane_ref, spec, ROWS, scratch)
     screen(spec, low_ref, wide_ref, column_ref, NG)
@@ -281,11 +281,13 @@
     same = lax.ppermute(code, axes, route(False))
     cross = lax.ppermute(wide, axes, route(True))
     beside = lax.ppermute(marked, "grid", swap)
-    other, top = call(near_kernel, (field, sent), same, orbitals, stacked, scratch=[work])
+    other, beyond, top = call(
+        near_kernel, (field, field, sent), same, cross, orbitals, stacked, scratch=[work]
+    )
     partner, top, beside_share, cross = call(
-        pair_kernel, (field, sent, sent, marks), cross, beside, top, *tables,
+        pair_kernel, (field, sent, sent, marks), beyond, beside, top, *tables,
         scratch=[
-            pltpu.VMEM((ROWS, PLANE), jnp.float32), spec, work,
+            spec, work,
             pltpu.VMEM((2, ROWS, PLANE), jnp.float32),
         ],
     )

time: 48.8 us -> 48.6 us (level)
  no operation moved by 1% of the time
where the time goes in v4:
time: 48.6 us; the launch traced here: 48.3 us
  starting transfers between devices  33.6 us (69%)
  waiting for transfers between devices  7.64 us (16%)
  Pallas kernels  4.87 us (10%)
  local copies, waits for them, and re-layouts  1.09 us (2%)
  other arithmetic  0.92 us (2%)
    ppermute x1, starting transfers between devices, on_device(): lax.ppermute(cross, axes, home(True))[:, :PLANE]  16.2 us
    ppermute x1, starting transfers between devices, on_device(): cross = lax.ppermute(wide, axes, route(True))  5.76 us
    pallas_call x6, Pallas kernels, call(): pl.pallas_call(kernel, out_shape=outs, in_specs=[vmem] * len(args), out_s...  4.87 us
    ppermute x1, starting transfers between devices, on_device(): same = lax.ppermute(code, axes, route(False))  4.04 us
    ppermute x1, waiting for transfers between devices, on_device(): same = lax.ppermute(code, axes, route(False))  3.29 us
    ppermute x1, waiting for transfers between devices, on_device(): lax.ppermute(beside_share, 'grid', swap)  3.03 us
    ppermute x1, starting transfers between devices, on_device(): beside = lax.ppermute(marked, 'grid', swap)  2.86 us
    ppermute x1, starting transfers between devices, on_device(): lax.ppermute(same, axes, home(False))  2.59 us
  transfers between devices with their start and end apart: 6, of which 3 were waited for; matrix products, arithmetic and copies ran while one was open for 0% of the time, Pallas kernels for 7%

profile of v4, /device:TPU:1, one launch (start us, length us, event | category | flops | bytes accessed | tf_op | source)
XLA Modules:
  0.0 48.3 jit_solution(14563243076918272206)
XLA Ops:
  0.0 0.0 copy-start
  0.0 1.0 %copy-done = f32[1,32,4096]{2,1,0:T(8,128)S(1)} copy-done((f32[1,32,4096]{2,1,0:T(8,128)S(1)}, f32[1,32,4096]{2,1,0:T(8,128)}, u32[]{:S(2)}) %copy-start) | copy-done | bytes 524312
  1.0 0.1 shard_map.55
  1.1 5.8 %collective-permute-start.2 = (bf16[32,4352]{1,0:T(8,128)(2,1)S(1)}, bf16[32,4352]{1,0:T(8,128)(2,1)S(1)}, u32[]{:S(2)}, u32[]{:S(2)}) collective-permute-start(bf16[32,4352]{1,0:T(8,128)(2,1)S(1)} %get-tuple-element.17), channel_id=1, source_target_pairs={{511,0},{508,1},{1,2},{510,3},{3,4},{0,5},{5,6},{2,7},{7,8},{4,9},... | collective-permute-start | bytes 835592 | tf_op jit(solution)/shard_map/ppermute | solution.py:282
  6.9 0.0 copy-start.2
  6.9 0.6 %shard_map.56.mine_ref = bf16[32,4224]{1,0:T(8,128)(2,1)S(1)} custom-call(f32[1,32,4096]{2,1,0:T(8,128)S(1)} %copy-done, bf16[32,4096]{1,0:T(8,128)(2,1)S(1)} %get-tuple-element.16.code_ref), custom_call_target="tpu_custom_call" | custom-call | tf_op jit(solution)/shard_map/pallas_call | solution.py:239
  7.5 0.0 copy-start.3
  7.5 0.0 copy-start.4
  7.5 0.0 copy-start.5
  7.5 2.9 %collective-permute-start = (bf16[32,4224]{1,0:T(8,128)(2,1)S(1)}, bf16[32,4224]{1,0:T(8,128)(2,1)S(1)}, u32[]{:S(2)}, u32[]{:S(2)}) collective-permute-start(bf16[32,4224]{1,0:T(8,128)(2,1)S(1)} %shard_map.56.mine_ref), channel_id=1, source_target_pairs={{0,1},{1,0},{2,3},{3,2},{4,5},{5,4},{6,7},{7,6},{8,9},{9,8},{10,11... | collective-permute-start | bytes 811016 | tf_op jit(solution)/shard_map/ppermute | solution.py:283
  10.4 4.0 %collective-permute-start.1 = (bf16[32,4096]{1,0:T(8,128)(2,1)S(1)}, bf16[32,4096]{1,0:T(8,128)(2,1)S(1)}, u32[]{:S(2)}, u32[]{:S(2)}) collective-permute-start(bf16[32,4096]{1,0:T(8,128)(2,1)S(1)} %get-tuple-element.16.code_ref), channel_id=1, source_target_pairs={{510,0},{509,1},{0,2},{511,3},{2,4},{1,5},{4,6},{3,7},{6,8},{5,9},... | collective-permute-start | bytes 786440 | tf_op jit(solution)/shard_map/ppermute | solution.py:281
  14.4 3.3 %collective-permute-done.1.same_ref = bf16[32,4096]{1,0:T(8,128)(2,1)S(1)} collective-permute-done((bf16[32,4096]{1,0:T(8,128)(2,1)S(1)}, bf16[32,4096]{1,0:T(8,128)(2,1)S(1)}, u32[]{:S(2)}, u32[]{:S(2)}) %collective-permute-start.1) | collective-permute-done | bytes 262176 | tf_op jit(solution)/shard_map/ppermute | solution.py:281
  17.7 0.0 collective-permute-done.2.cross_ref
  17.7 0.0 copy-done.2
  17.7 0.6 %shard_map.57 = (f32[32,4096]{1,0:T(8,128)S(1)}, f32[32,4096]{1,0:T(8,128)S(1)}, bf16[32,4096]{1,0:T(8,128)(2,1)S(1)}) custom-call(bf16[32,4096]{1,0:T(8,128)(2,1)S(1)} %collective-permute-done.1.same_ref, bf16[32,4352]{1,0:T(8,128)(2,1)S(1)} %collective-permute-done.2.cross_ref, f32[1,32,4096]{2,1,0:T(8,128)S(1)} %copy-done, bf16[256,256]{1,0:T(8,128)(2,1)S(1)} %copy-done.2), custom_call_target="tpu_custom_call" | custom-call | tf_op jit(solution)/shard_map/pallas_call | solution.py:239
  18.3 0.0 collective-permute-done.beside_code
  18.3 0.0 copy-done.3
  18.3 0.0 copy-done.4
  18.3 0.0 copy-done.5
  18.3 0.0 copy-start.1
  18.4 1.5 %shard_map.58 = (f32[32,4096]{1,0:T(8,128)S(1)}, bf16[32,4096]{1,0:T(8,128)(2,1)S(1)}, bf16[32,4096]{1,0:T(8,128)(2,1)S(1)}, bf16[32,4224]{1,0:T(8,128)(2,1)S(1)}) custom-call(f32[32,4096]{1,0:T(8,128)S(1)} %get-tuple-element.18.other, bf16[32,4224]{1,0:T(8,128)(2,1)S(1)} %collective-permute-done.beside_code, ...), custom_call_target="tpu_custom_call" | custom-call | tf_op jit(solution)/shard_map/pallas_call | solution.py:239
  19.9 16.2 %collective-permute-start.3 = (bf16[32,4224]{1,0:T(8,128)(2,1)S(1)}, bf16[32,4224]{1,0:T(8,128)(2,1)S(1)}, u32[]{:S(2)}, u32[]{:S(2)}) collective-permute-start(bf16[32,4224]{1,0:T(8,128)(2,1)S(1)} %get-tuple-element.24), channel_id=1, source_target_pairs={{0,511},{1,508},{2,1},{3,510},{4,3},{5,0},{6,5},{7,2},{8,7},{9,4},... | collective-permute-start | bytes 811016 | tf_op jit(solution)/shard_map/ppermute | solution.py:303
  36.1 0.0 copy-done.1
  36.1 0.5 %shard_map.59 = (f32[32,4096]{1,0:T(8,128)S(1)}, bf16[32,4096]{1,0:T(8,128)(2,1)S(1)}) custom-call(bf16[32,4096]{1,0:T(8,128)(2,1)S(1)} %get-tuple-element.21.spec_ref, bf16[256,256]{1,0:T(8,128)(2,1)S(1)} %copy-done.2, f32[1,32,4096]{2,1,0:T(8,128)S(1)} %copy-done.1, f32[32,4096]{1,0:T(8,128)S(1)} %get-tuple-element.22.other_ref), custom_call_target="tpu_custom_call" | custom-call | tf_op jit(solution)/shard_map/pallas_call | solution.py:239
  36.6 2.6 %collective-permute-start.5 = (bf16[32,4096]{1,0:T(8,128)(2,1)S(1)}, bf16[32,4096]{1,0:T(8,128)(2,1)S(1)}, u32[]{:S(2)}, u32[]{:S(2)}) collective-permute-start(bf16[32,4096]{1,0:T(8,128)(2,1)S(1)} %get-tuple-element.26), channel_id=1, source_target_pairs={{0,510},{1,509},{2,0},{3,511},{4,2},{5,1},{6,4},{7,3},{8,6},{9,5},... | collective-permute-start | bytes 786440 | tf_op jit(solution)/shard_map/ppermute | solution.py:305
  39.2 2.1 %collective-permute-start.4 = (bf16[32,4096]{1,0:T(8,128)(2,1)S(1)}, bf16[32,4096]{1,0:T(8,128)(2,1)S(1)}, u32[]{:S(2)}, u32[]{:S(2)}) collective-permute-start(bf16[32,4096]{1,0:T(8,128)(2,1)S(1)} %get-tuple-element.25), channel_id=1, source_target_pairs={{0,1},{1,0},{2,3},{3,2},{4,5},{5,4},{6,7},{7,6},{8,9},{9,8},{10,11... | collective-permute-start | bytes 786440 | tf_op jit(solution)/shard_map/ppermute | solution.py:304
  41.3 1.7 %shard_map.60 = f32[32,4096]{1,0:T(8,128)S(1)} custom-call(f32[1,32,4096]{2,1,0:T(8,128)S(1)} %copy-done.1, bf16[32,4224]{1,0:T(8,128)(2,1)S(1)} %shard_map.56.mine_ref, bf16[32,4224]{1,0:T(8,128)(2,1)S(1)} %collective-permute-done.beside_code, f32[32,4096]{1,0:T(8,128)S(1)} %get-tuple-element.20.field_ref, bf16[256,256]{1,0:T(8,128)(2,1)S(1)} %copy-done.2, ...), custom_call_target="tpu_custom_call" | custom-call | tf_op jit(solution)/shard_map/pallas_call | solution.py:239
  43.0 1.3 %collective-permute-done.5 = bf16[32,4096]{1,0:T(8,128)(2,1)S(1)} collective-permute-done((bf16[32,4096]{1,0:T(8,128)(2,1)S(1)}, bf16[32,4096]{1,0:T(8,128)(2,1)S(1)}, u32[]{:S(2)}, u32[]{:S(2)}) %collective-permute-start.5) | collective-permute-done | bytes 262176 | tf_op jit(solution)/shard_map/ppermute | solution.py:305
  44.3 3.0 %collective-permute-done.4 = bf16[32,4096]{1,0:T(8,128)(2,1)S(1)} collective-permute-done((bf16[32,4096]{1,0:T(8,128)(2,1)S(1)}, bf16[32,4096]{1,0:T(8,128)(2,1)S(1)}, u32[]{:S(2)}, u32[]{:S(2)}) %collective-permute-start.4) | collective-permute-done | bytes 262176 | tf_op jit(solution)/shard_map/ppermute | solution.py:304
  47.3 0.0 collective-permute-done.3
  47.3 0.9 %negate_bitcast_fusion = f32[1,32,4096]{2,1,0:T(8,128)} fusion(bf16[32,4096]{1,0:T(8,128)(2,1)S(1)} %collective-permute-done.5, bf16[32,4096]{1,0:T(8,128)(2,1)S(1)} %collective-permute-done.4, f32[32,4096]{1,0:T(8,128)S(1)} %shard_map.60, bf16[32,4224]{1,0:T(8,128)(2,1)S(1)} %collective-permute-done.3), kind=kLoop, calls=%fused_computation | loop fusion | flops 917504 | bytes 1835008 | tf_op jit(solution)/shard_map/neg | solution.py:308
Async XLA Ops:
  0.0 1.0 %copy-start = (f32[1,32,4096]{2,1,0:T(8,128)S(1)}, f32[1,32,4096]{2,1,0:T(8,128)}, u32[]{:S(2)}) copy-start(f32[1,32,4096]{2,1,0:T(8,128)} %psi_ref.9) | copy-start | bytes 1572868
  1.1 16.6 %collective-permute-start.2 = (bf16[32,4352]{1,0:T(8,128)(2,1)S(1)}, bf16[32,4352]{1,0:T(8,128)(2,1)S(1)}, u32[]{:S(2)}, u32[]{:S(2)}) collective-permute-start(bf16[32,4352]{1,0:T(8,128)(2,1)S(1)} %get-tuple-element.17), channel_id=1, source_target_pairs={{511,0},{508,1},{1,2},{510,3},{3,4},{0,5},{5,6},{2,7},{7,8},{4,9},... | collective-permute-start | bytes 835592 | tf_op jit(solution)/shard_map/ppermute | solution.py:282
  6.9 10.8 %copy-start.2 = (bf16[256,256]{1,0:T(8,128)(2,1)S(1)}, bf16[256,256]{1,0:T(8,128)(2,1)}, u32[]{:S(2)}) copy-start(bf16[256,256]{1,0:T(8,128)(2,1)} %constant.13.plane_ref) | copy-start | bytes 393220
  7.5 10.9 %copy-start.3 = (bf16[64,192]{1,0:T(8,128)(2,1)S(1)}, bf16[64,192]{1,0:T(8,128)(2,1)}, u32[]{:S(2)}) copy-start(bf16[64,192]{1,0:T(8,128)(2,1)} %constant.10.clone.wide_ref) | copy-start | bytes 73732
  7.5 10.9 %copy-start.4 = (f32[1,4096]{1,0:T(1,128)S(1)}, f32[1,4096]{1,0:T(1,128)}, u32[]{:S(2)}) copy-start(f32[1,4096]{1,0:T(1,128)} %constant.11.clone.column_ref) | copy-start | bytes 49156
  7.5 10.8 %copy-start.5 = (bf16[64,64]{1,0:T(8,128)(2,1)S(1)}, bf16[64,64]{1,0:T(8,128)(2,1)}, u32[]{:S(2)}) copy-start(bf16[64,64]{1,0:T(8,128)(2,1)} %constant.9.clone.low_ref) | copy-start | bytes 24580
  7.5 10.8 %collective-permute-start = (bf16[32,4224]{1,0:T(8,128)(2,1)S(1)}, bf16[32,4224]{1,0:T(8,128)(2,1)S(1)}, u32[]{:S(2)}, u32[]{:S(2)}) collective-permute-start(bf16[32,4224]{1,0:T(8,128)(2,1)S(1)} %shard_map.56.mine_ref), channel_id=1, source_target_pairs={{0,1},{1,0},{2,3},{3,2},{4,5},{5,4},{6,7},{7,6},{8,9},{9,8},{10,11... | collective-permute-start | bytes 811016 | tf_op jit(solution)/shard_map/ppermute | solution.py:283
  10.4 7.3 %collective-permute-start.1 = (bf16[32,4096]{1,0:T(8,128)(2,1)S(1)}, bf16[32,4096]{1,0:T(8,128)(2,1)S(1)}, u32[]{:S(2)}, u32[]{:S(2)}) collective-permute-start(bf16[32,4096]{1,0:T(8,128)(2,1)S(1)} %get-tuple-element.16.code_ref), channel_id=1, source_target_pairs={{510,0},{509,1},{0,2},{511,3},{2,4},{1,5},{4,6},{3,7},{6,8},{5,9},... | collective-permute-start | bytes 786440 | tf_op jit(solution)/shard_map/ppermute | solution.py:281
  18.3 17.8 %copy-start.1 = (f32[1,32,4096]{2,1,0:T(8,128)S(1)}, f32[1,32,4096]{2,1,0:T(8,128)}, u32[]{:S(2)}) copy-start(f32[1,32,4096]{2,1,0:T(8,128)} %psi_ref.9) | copy-start | bytes 1572868
  19.9 27.5 %collective-permute-start.3 = (bf16[32,4224]{1,0:T(8,128)(2,1)S(1)}, bf16[32,4224]{1,0:T(8,128)(2,1)S(1)}, u32[]{:S(2)}, u32[]{:S(2)}) collective-permute-start(bf16[32,4224]{1,0:T(8,128)(2,1)S(1)} %get-tuple-element.24), channel_id=1, source_target_pairs={{0,511},{1,508},{2,1},{3,510},{4,3},{5,0},{6,5},{7,2},{8,7},{9,4},... | collective-permute-start | bytes 811016 | tf_op jit(solution)/shard_map/ppermute | solution.py:303
  36.6 7.7 %collective-permute-start.5 = (bf16[32,4096]{1,0:T(8,128)(2,1)S(1)}, bf16[32,4096]{1,0:T(8,128)(2,1)S(1)}, u32[]{:S(2)}, u32[]{:S(2)}) collective-permute-start(bf16[32,4096]{1,0:T(8,128)(2,1)S(1)} %get-tuple-element.26), channel_id=1, source_target_pairs={{0,510},{1,509},{2,0},{3,511},{4,2},{5,1},{6,4},{7,3},{8,6},{9,5},... | collective-permute-start | bytes 786440 | tf_op jit(solution)/shard_map/ppermute | solution.py:305
  39.2 8.1 %collective-permute-start.4 = (bf16[32,4096]{1,0:T(8,128)(2,1)S(1)}, bf16[32,4096]{1,0:T(8,128)(2,1)S(1)}, u32[]{:S(2)}, u32[]{:S(2)}) collective-permute-start(bf16[32,4096]{1,0:T(8,128)(2,1)S(1)} %get-tuple-element.25), channel_id=1, source_target_pairs={{0,1},{1,0},{2,3},{3,2},{4,5},{5,4},{6,7},{7,6},{8,9},{9,8},{10,11... | collective-permute-start | bytes 786440 | tf_op jit(solution)/shard_map/ppermute | solution.py:304

commit v5 on v4

--- a/solution.py
+++ b/solution.py
@@ -16,8 +16,8 @@
 LANES = 2 * NG
 BLOCKS = PLANE // LANES
 CODE = 64.0
-CHUNK = 16
-WIDTH = 2048
+CHUNK = 32
+WIDTH = 4096
 coulomb = 46.9 * 46.9 / math.pi
 
 

time: 48.6 us -> 48.5 us (level)
  no operation moved by 1% of the time
where the time goes in v5:
time: 48.5 us; the launch traced here: 48.2 us
  starting transfers between devices  33.6 us (69%)
  waiting for transfers between devices  7.47 us (15%)
  Pallas kernels  4.96 us (10%)
  local copies, waits for them, and re-layouts  1.09 us (2%)
  other arithmetic  0.92 us (2%)
    ppermute x1, starting transfers between devices, on_device(): lax.ppermute(cross, axes, home(True))[:, :PLANE]  16.3 us
    ppermute x1, starting transfers between devices, on_device(): cross = lax.ppermute(wide, axes, route(True))  5.76 us
    pallas_call x6, Pallas kernels, call(): pl.pallas_call(kernel, out_shape=outs, in_specs=[vmem] * len(args), out_s...  4.96 us
    ppermute x1, starting transfers between devices, on_device(): same = lax.ppermute(code, axes, route(False))  4.04 us
    ppermute x1, waiting for transfers between devices, on_device(): same = lax.ppermute(code, axes, route(False))  3.29 us
    ppermute x1, waiting for transfers between devices, on_device(): lax.ppermute(beside_share, 'grid', swap)  3 us
    ppermute x1, starting transfers between devices, on_device(): beside = lax.ppermute(marked, 'grid', swap)  2.86 us
    ppermute x1, starting transfers between devices, on_device(): lax.ppermute(same, axes, home(False))  2.56 us
  transfers between devices with their start and end apart: 6, of which 3 were waited for; matrix products, arithmetic and copies ran while one was open for 0% of the time, Pallas kernels for 7%

profile of v5, /device:TPU:1, one launch (start us, length us, event | category | flops | bytes accessed | tf_op | source)
XLA Modules:
  0.0 48.2 jit_solution(17185867151953527260)
XLA Ops:
  0.0 0.0 copy-start
  0.0 1.0 %copy-done = f32[1,32,4096]{2,1,0:T(8,128)S(1)} copy-done((f32[1,32,4096]{2,1,0:T(8,128)S(1)}, f32[1,32,4096]{2,1,0:T(8,128)}, u32[]{:S(2)}) %copy-start) | copy-done | bytes 524312
  1.0 0.1 shard_map.55
  1.1 5.8 %collective-permute-start.2 = (bf16[32,4352]{1,0:T(8,128)(2,1)S(1)}, bf16[32,4352]{1,0:T(8,128)(2,1)S(1)}, u32[]{:S(2)}, u32[]{:S(2)}) collective-permute-start(bf16[32,4352]{1,0:T(8,128)(2,1)S(1)} %get-tuple-element.17), channel_id=1, source_target_pairs={{511,0},{508,1},{1,2},{510,3},{3,4},{0,5},{5,6},{2,7},{7,8},{4,9},... | collective-permute-start | bytes 835592 | tf_op jit(solution)/shard_map/ppermute | solution.py:282
  6.9 0.0 copy-start.2
  6.9 0.6 %shard_map.56.mine_ref = bf16[32,4224]{1,0:T(8,128)(2,1)S(1)} custom-call(f32[1,32,4096]{2,1,0:T(8,128)S(1)} %copy-done, bf16[32,4096]{1,0:T(8,128)(2,1)S(1)} %get-tuple-element.16.code_ref), custom_call_target="tpu_custom_call" | custom-call | tf_op jit(solution)/shard_map/pallas_call | solution.py:239
  7.5 0.0 copy-start.3
  7.5 0.0 copy-start.4
  7.5 0.0 copy-start.5
  7.5 2.9 %collective-permute-start = (bf16[32,4224]{1,0:T(8,128)(2,1)S(1)}, bf16[32,4224]{1,0:T(8,128)(2,1)S(1)}, u32[]{:S(2)}, u32[]{:S(2)}) collective-permute-start(bf16[32,4224]{1,0:T(8,128)(2,1)S(1)} %shard_map.56.mine_ref), channel_id=1, source_target_pairs={{0,1},{1,0},{2,3},{3,2},{4,5},{5,4},{6,7},{7,6},{8,9},{9,8},{10,11... | collective-permute-start | bytes 811016 | tf_op jit(solution)/shard_map/ppermute | solution.py:283
  10.4 4.0 %collective-permute-start.1 = (bf16[32,4096]{1,0:T(8,128)(2,1)S(1)}, bf16[32,4096]{1,0:T(8,128)(2,1)S(1)}, u32[]{:S(2)}, u32[]{:S(2)}) collective-permute-start(bf16[32,4096]{1,0:T(8,128)(2,1)S(1)} %get-tuple-element.16.code_ref), channel_id=1, source_target_pairs={{510,0},{509,1},{0,2},{511,3},{2,4},{1,5},{4,6},{3,7},{6,8},{5,9},... | collective-permute-start | bytes 786440 | tf_op jit(solution)/shard_map/ppermute | solution.py:281
  14.4 3.3 %collective-permute-done.1.same_ref = bf16[32,4096]{1,0:T(8,128)(2,1)S(1)} collective-permute-done((bf16[32,4096]{1,0:T(8,128)(2,1)S(1)}, bf16[32,4096]{1,0:T(8,128)(2,1)S(1)}, u32[]{:S(2)}, u32[]{:S(2)}) %collective-permute-start.1) | collective-permute-done | bytes 262176 | tf_op jit(solution)/shard_map/ppermute | solution.py:281
  17.7 0.0 collective-permute-done.2.cross_ref
  17.7 0.0 copy-done.2
  17.7 0.6 %shard_map.57 = (f32[32,4096]{1,0:T(8,128)S(1)}, f32[32,4096]{1,0:T(8,128)S(1)}, bf16[32,4096]{1,0:T(8,128)(2,1)S(1)}) custom-call(bf16[32,4096]{1,0:T(8,128)(2,1)S(1)} %collective-permute-done.1.same_ref, bf16[32,4352]{1,0:T(8,128)(2,1)S(1)} %collective-permute-done.2.cross_ref, f32[1,32,4096]{2,1,0:T(8,128)S(1)} %copy-done, bf16[256,256]{1,0:T(8,128)(2,1)S(1)} %copy-done.2), custom_call_target="tpu_custom_call" | custom-call | tf_op jit(solution)/shard_map/pallas_call | solution.py:239
  18.3 0.0 collective-permute-done.beside_code
  18.3 0.0 copy-done.3
  18.3 0.0 copy-done.4
  18.3 0.0 copy-done.5
  18.3 0.0 copy-start.1
  18.4 1.4 %shard_map.58 = (f32[32,4096]{1,0:T(8,128)S(1)}, bf16[32,4096]{1,0:T(8,128)(2,1)S(1)}, bf16[32,4096]{1,0:T(8,128)(2,1)S(1)}, bf16[32,4224]{1,0:T(8,128)(2,1)S(1)}) custom-call(f32[32,4096]{1,0:T(8,128)S(1)} %get-tuple-element.18.other, bf16[32,4224]{1,0:T(8,128)(2,1)S(1)} %collective-permute-done.beside_code, ...), custom_call_target="tpu_custom_call" | custom-call | tf_op jit(solution)/shard_map/pallas_call | solution.py:239
  19.8 16.3 %collective-permute-start.3 = (bf16[32,4224]{1,0:T(8,128)(2,1)S(1)}, bf16[32,4224]{1,0:T(8,128)(2,1)S(1)}, u32[]{:S(2)}, u32[]{:S(2)}) collective-permute-start(bf16[32,4224]{1,0:T(8,128)(2,1)S(1)} %get-tuple-element.24), channel_id=1, source_target_pairs={{0,511},{1,508},{2,1},{3,510},{4,3},{5,0},{6,5},{7,2},{8,7},{9,4},... | collective-permute-start | bytes 811016 | tf_op jit(solution)/shard_map/ppermute | solution.py:303
  36.1 0.0 copy-done.1
  36.1 0.5 shard_map.59
  36.6 2.6 %collective-permute-start.5 = (bf16[32,4096]{1,0:T(8,128)(2,1)S(1)}, bf16[32,4096]{1,0:T(8,128)(2,1)S(1)}, u32[]{:S(2)}, u32[]{:S(2)}) collective-permute-start(bf16[32,4096]{1,0:T(8,128)(2,1)S(1)} %get-tuple-element.26), channel_id=1, source_target_pairs={{0,510},{1,509},{2,0},{3,511},{4,2},{5,1},{6,4},{7,3},{8,6},{9,5},... | collective-permute-start | bytes 786440 | tf_op jit(solution)/shard_map/ppermute | solution.py:305
  39.2 2.1 %collective-permute-start.4 = (bf16[32,4096]{1,0:T(8,128)(2,1)S(1)}, bf16[32,4096]{1,0:T(8,128)(2,1)S(1)}, u32[]{:S(2)}, u32[]{:S(2)}) collective-permute-start(bf16[32,4096]{1,0:T(8,128)(2,1)S(1)} %get-tuple-element.25), channel_id=1, source_target_pairs={{0,1},{1,0},{2,3},{3,2},{4,5},{5,4},{6,7},{7,6},{8,9},{9,8},{10,11... | collective-permute-start | bytes 786440 | tf_op jit(solution)/shard_map/ppermute | solution.py:304
  41.3 1.8 %shard_map.60 = f32[32,4096]{1,0:T(8,128)S(1)} custom-call(f32[1,32,4096]{2,1,0:T(8,128)S(1)} %copy-done.1, bf16[32,4224]{1,0:T(8,128)(2,1)S(1)} %shard_map.56.mine_ref, bf16[32,4224]{1,0:T(8,128)(2,1)S(1)} %collective-permute-done.beside_code, f32[32,4096]{1,0:T(8,128)S(1)} %get-tuple-element.20.field_ref, bf16[256,256]{1,0:T(8,128)(2,1)S(1)} %copy-done.2, ...), custom_call_target="tpu_custom_call" | custom-call | tf_op jit(solution)/shard_map/pallas_call | solution.py:239
  43.1 1.2 %collective-permute-done.5 = bf16[32,4096]{1,0:T(8,128)(2,1)S(1)} collective-permute-done((bf16[32,4096]{1,0:T(8,128)(2,1)S(1)}, bf16[32,4096]{1,0:T(8,128)(2,1)S(1)}, u32[]{:S(2)}, u32[]{:S(2)}) %collective-permute-start.5) | collective-permute-done | bytes 262176 | tf_op jit(solution)/shard_map/ppermute | solution.py:305
  44.3 3.0 %collective-permute-done.4 = bf16[32,4096]{1,0:T(8,128)(2,1)S(1)} collective-permute-done((bf16[32,4096]{1,0:T(8,128)(2,1)S(1)}, bf16[32,4096]{1,0:T(8,128)(2,1)S(1)}, u32[]{:S(2)}, u32[]{:S(2)}) %collective-permute-start.4) | collective-permute-done | bytes 262176 | tf_op jit(solution)/shard_map/ppermute | solution.py:304
  47.3 0.0 collective-permute-done.3
  47.3 0.9 %negate_bitcast_fusion = f32[1,32,4096]{2,1,0:T(8,128)} fusion(bf16[32,4096]{1,0:T(8,128)(2,1)S(1)} %collective-permute-done.5, bf16[32,4096]{1,0:T(8,128)(2,1)S(1)} %collective-permute-done.4, f32[32,4096]{1,0:T(8,128)S(1)} %shard_map.60, bf16[32,4224]{1,0:T(8,128)(2,1)S(1)} %collective-permute-done.3), kind=kLoop, calls=%fused_computation | loop fusion | flops 917504 | bytes 1835008 | tf_op jit(solution)/shard_map/neg | solution.py:308
Async XLA Ops:
  0.0 1.0 %copy-start = (f32[1,32,4096]{2,1,0:T(8,128)S(1)}, f32[1,32,4096]{2,1,0:T(8,128)}, u32[]{:S(2)}) copy-start(f32[1,32,4096]{2,1,0:T(8,128)} %psi_ref.9) | copy-start | bytes 1572868
  1.1 16.6 %collective-permute-start.2 = (bf16[32,4352]{1,0:T(8,128)(2,1)S(1)}, bf16[32,4352]{1,0:T(8,128)(2,1)S(1)}, u32[]{:S(2)}, u32[]{:S(2)}) collective-permute-start(bf16[32,4352]{1,0:T(8,128)(2,1)S(1)} %get-tuple-element.17), channel_id=1, source_target_pairs={{511,0},{508,1},{1,2},{510,3},{3,4},{0,5},{5,6},{2,7},{7,8},{4,9},... | collective-permute-start | bytes 835592 | tf_op jit(solution)/shard_map/ppermute | solution.py:282
  6.9 10.8 %copy-start.2 = (bf16[256,256]{1,0:T(8,128)(2,1)S(1)}, bf16[256,256]{1,0:T(8,128)(2,1)}, u32[]{:S(2)}) copy-start(bf16[256,256]{1,0:T(8,128)(2,1)} %constant.13.plane_ref) | copy-start | bytes 393220
  7.5 10.9 %copy-start.3 = (bf16[64,192]{1,0:T(8,128)(2,1)S(1)}, bf16[64,192]{1,0:T(8,128)(2,1)}, u32[]{:S(2)}) copy-start(bf16[64,192]{1,0:T(8,128)(2,1)} %constant.10.clone.wide_ref) | copy-start | bytes 73732
  7.5 10.9 %copy-start.4 = (f32[1,4096]{1,0:T(1,128)S(1)}, f32[1,4096]{1,0:T(1,128)}, u32[]{:S(2)}) copy-start(f32[1,4096]{1,0:T(1,128)} %constant.11.clone.column_ref) | copy-start | bytes 49156
  7.5 10.8 %copy-start.5 = (bf16[64,64]{1,0:T(8,128)(2,1)S(1)}, bf16[64,64]{1,0:T(8,128)(2,1)}, u32[]{:S(2)}) copy-start(bf16[64,64]{1,0:T(8,128)(2,1)} %constant.9.clone.low_ref) | copy-start | bytes 24580
  7.5 10.8 %collective-permute-start = (bf16[32,4224]{1,0:T(8,128)(2,1)S(1)}, bf16[32,4224]{1,0:T(8,128)(2,1)S(1)}, u32[]{:S(2)}, u32[]{:S(2)}) collective-permute-start(bf16[32,4224]{1,0:T(8,128)(2,1)S(1)} %shard_map.56.mine_ref), channel_id=1, source_target_pairs={{0,1},{1,0},{2,3},{3,2},{4,5},{5,4},{6,7},{7,6},{8,9},{9,8},{10,11... | collective-permute-start | bytes 811016 | tf_op jit(solution)/shard_map/ppermute | solution.py:283
  10.4 7.3 %collective-permute-start.1 = (bf16[32,4096]{1,0:T(8,128)(2,1)S(1)}, bf16[32,4096]{1,0:T(8,128)(2,1)S(1)}, u32[]{:S(2)}, u32[]{:S(2)}) collective-permute-start(bf16[32,4096]{1,0:T(8,128)(2,1)S(1)} %get-tuple-element.16.code_ref), channel_id=1, source_target_pairs={{510,0},{509,1},{0,2},{511,3},{2,4},{1,5},{4,6},{3,7},{6,8},{5,9},... | collective-permute-start | bytes 786440 | tf_op jit(solution)/shard_map/ppermute | solution.py:281
  18.3 17.7 %copy-start.1 = (f32[1,32,4096]{2,1,0:T(8,128)S(1)}, f32[1,32,4096]{2,1,0:T(8,128)}, u32[]{:S(2)}) copy-start(f32[1,32,4096]{2,1,0:T(8,128)} %psi_ref.9) | copy-start | bytes 1572868
  19.8 27.5 %collective-permute-start.3 = (bf16[32,4224]{1,0:T(8,128)(2,1)S(1)}, bf16[32,4224]{1,0:T(8,128)(2,1)S(1)}, u32[]{:S(2)}, u32[]{:S(2)}) collective-permute-start(bf16[32,4224]{1,0:T(8,128)(2,1)S(1)} %get-tuple-element.24), channel_id=1, source_target_pairs={{0,511},{1,508},{2,1},{3,510},{4,3},{5,0},{6,5},{7,2},{8,7},{9,4},... | collective-permute-start | bytes 811016 | tf_op jit(solution)/shard_map/ppermute | solution.py:303
  36.6 7.7 %collective-permute-start.5 = (bf16[32,4096]{1,0:T(8,128)(2,1)S(1)}, bf16[32,4096]{1,0:T(8,128)(2,1)S(1)}, u32[]{:S(2)}, u32[]{:S(2)}) collective-permute-start(bf16[32,4096]{1,0:T(8,128)(2,1)S(1)} %get-tuple-element.26), channel_id=1, source_target_pairs={{0,510},{1,509},{2,0},{3,511},{4,2},{5,1},{6,4},{7,3},{8,6},{9,5},... | collective-permute-start | bytes 786440 | tf_op jit(solution)/shard_map/ppermute | solution.py:305
  39.2 8.1 %collective-permute-start.4 = (bf16[32,4096]{1,0:T(8,128)(2,1)S(1)}, bf16[32,4096]{1,0:T(8,128)(2,1)S(1)}, u32[]{:S(2)}, u32[]{:S(2)}) collective-permute-start(bf16[32,4096]{1,0:T(8,128)(2,1)S(1)} %get-tuple-element.25), channel_id=1, source_target_pairs={{0,1},{1,0},{2,3},{3,2},{4,5},{5,4},{6,7},{7,6},{8,9},{9,8},{10,11... | collective-permute-start | bytes 786440 | tf_op jit(solution)/shard_map/ppermute | solution.py:304
